TPU v7x, 512 devices: a whole 4x4x16 slice. The times are simulated.
512 devices in a mesh: section: 16 (over z_hi, x), dp: 32 (over z_lo, y, core).
Axes of the slice: x: 4, y: 4, z: 16 (z_hi: 4, z_lo: 4; z = z_hi * 4 + z_lo), core: 2. Of those that a mesh axis runs over, the one named last changes fastest.
Arguments:
- boundary_in: bfloat16 [8192, 640], P('dp'), may hold values from -6 to 6
- weights: bfloat16 [16, 2560, 640], P('section', 'dp'), may hold values from -0.125 to 0.125
- gains: float32 [16, 2560], P('section'), may hold values from 0.5 to 2
- cotangent: bfloat16 [8192, 640], P('dp'), may hold values from -6 to 6
Outputs:
- weight_grad: float32 [16, 2560, 640], P('section', 'dp')
- section_grad: bfloat16 [16, 8192, 640], P('section', 'dp')
All inputs are finite; a program needn't handle non-finite values.
Results may differ from a plain program's by a relative error of at most 0.035.
Values may be sent and summed in bfloat16 or wider, within the bound.
A program may use at most 64 MiB of HBM per device.

v0:
```python
import math

import jax
import jax.numpy as jnp
from jax import lax
from jax.sharding import PartitionSpec as P

MICRO = 4


def from_behind(shard, axis, by):
    peers = lax.axis_size(axis)
    pairs = [(i, i + by) for i in range(peers) if 0 <= i + by < peers]
    return lax.ppermute(shard, axis, pairs)


def activate(pre_norm, gain_row):
    inv_rms = lax.rsqrt(jnp.mean(pre_norm * pre_norm, axis=1, keepdims=True) + 1e-05)
    normed = pre_norm * inv_rms * gain_row
    return (inv_rms, normed, jax.nn.silu(normed).astype(jnp.bfloat16))


def section_forward(block_input, weight, gain_row):
    pre_norm = jnp.einsum("rc,hc->rh", block_input, weight, preferred_element_type=jnp.float32)
    inv_rms, normed, activated = activate(pre_norm, gain_row)
    block_output = (
        block_input.astype(jnp.float32)
        + jnp.dot(activated, weight, preferred_element_type=jnp.float32)
    ).astype(jnp.bfloat16)
    return (pre_norm, block_output)


def section_backward(grad_out, pre_norm, weight, gain_row):
    inv_rms, normed, activated = activate(pre_norm, gain_row)
    grad_act = jnp.einsum("rc,hc->rh", grad_out, weight, preferred_element_type=jnp.float32)
    sigmoid_h = jax.nn.sigmoid(normed)
    grad_normed = grad_act * sigmoid_h * (1.0 + normed * (1.0 - sigmoid_h)) * gain_row
    grad_pre = (
        inv_rms
        * (
            grad_normed
            - pre_norm * inv_rms * inv_rms * jnp.mean(grad_normed * pre_norm, axis=1, keepdims=True)
        )
    ).astype(jnp.bfloat16)
    grad_in = (
        grad_out.astype(jnp.float32) + jnp.dot(grad_pre, weight, preferred_element_type=jnp.float32)
    ).astype(jnp.bfloat16)
    return (activated, grad_pre, grad_in)


def put_rows(store, values, row_start):
    return lax.dynamic_update_slice_in_dim(store, values, row_start, 0)


def take_rows(store, row_start, row_total):
    return lax.dynamic_slice_in_dim(store, row_start, row_total, 0)


def outer_sum(left, right):
    return jnp.einsum("rh,rc->hc", left, right, preferred_element_type=jnp.float32)


def shards(boundary_in, weights, gains, cotangent):
    sections = lax.axis_size("section")
    position = lax.axis_index("section")
    weight = lax.all_gather(weights, "dp", axis=1, tiled=True)[0]
    gain_row = gains[0]
    row_count, comp_width = boundary_in.shape
    hidden = weight.shape[0]
    block_rows = row_count // MICRO
    empty_block = jnp.zeros((block_rows, comp_width), jnp.bfloat16)

    def block_start(micro_index):
        return jnp.clip(micro_index, 0, MICRO - 1) * block_rows

    def forward_step(micro_index, incoming, stores):
        active = (micro_index >= 0) & (micro_index < MICRO)
        row_start = block_start(micro_index)
        first_block = take_rows(boundary_in, row_start, block_rows)
        block_input = jnp.where(position == 0, first_block, incoming)

        def forward_run_block(held_state):
            pre_norm, block_output = section_forward(block_input, weight, gain_row)
            saved = (
                put_rows(held_state[0], block_input, row_start),
                put_rows(held_state[1], pre_norm, row_start),
            )
            return (saved + held_state[2:], block_output)

        def forward_skip_block(held_state):
            return (held_state, empty_block)

        return lax.cond(active, forward_run_block, forward_skip_block, stores)

    def backward_step(micro_index, incoming, stores):
        active = (micro_index >= 0) & (micro_index < MICRO)
        row_start = block_start(micro_index)
        cot_block = take_rows(cotangent, row_start, block_rows)
        grad_out = jnp.where(position == sections - 1, cot_block, incoming)

        def backward_run_block(held_state):
            block_input = take_rows(held_state[0], row_start, block_rows)
            pre_norm = take_rows(held_state[1], row_start, block_rows)
            activated, grad_pre, grad_in = section_backward(grad_out, pre_norm, weight, gain_row)
            grad_store = put_rows(held_state[2], grad_in, row_start)
            grad_parts = (
                held_state[3] + outer_sum(grad_pre, block_input) + outer_sum(activated, grad_out),
            )
            return ((held_state[0], held_state[1], grad_store) + grad_parts, grad_in)

        def backward_skip_block(held_state):
            return (held_state, empty_block)

        return lax.cond(active, backward_run_block, backward_skip_block, stores)

    grad_parts = (jnp.zeros((hidden, comp_width), jnp.float32),)
    stores = (
        jnp.zeros((row_count, comp_width), jnp.bfloat16),
        jnp.zeros((row_count, hidden), jnp.float32),
        jnp.zeros((row_count, comp_width), jnp.bfloat16),
    ) + grad_parts

    def forward_tick(tick_index, loop_state):
        incoming, held_state = loop_state
        held_state, block_output = forward_step(tick_index - position, incoming, held_state)
        return (from_behind(block_output, "section", 1), held_state)

    def backward_tick(tick_index, loop_state):
        incoming, held_state = loop_state
        held_state, grad_in = backward_step(
            tick_index - (sections - 1 - position), incoming, held_state
        )
        return (from_behind(grad_in, "section", -1), held_state)

    loop_state = lax.fori_loop(0, MICRO + sections - 1, forward_tick, (empty_block, stores))
    loop_state = lax.fori_loop(0, MICRO + sections - 1, backward_tick, (empty_block, loop_state[1]))
    stores = loop_state[1]
    grad_store = stores[2]
    weight_sum = lax.psum_scatter(
        stores[3].astype(jnp.bfloat16), "dp", scatter_dimension=0, tiled=True
    ).astype(jnp.float32)
    weight_grad = (weight_sum / math.sqrt(row_count * lax.axis_size("dp")))[None]
    return (weight_grad, grad_store[None])


def solution(mesh):
    return jax.shard_map(
        shards,
        mesh=mesh,
        in_specs=(P("dp", None), P("section", "dp", None), P("section", None), P("dp", None)),
        out_specs=(P("section", "dp", None), P("section", "dp", None)),
        check_vma=False,
    )
```

profile of v0, /device:TPU:1, one launch (start us, length us, event | category | flops | bytes accessed | tf_op | source)
XLA Modules:
  0.0 990.1 jit_solution(6041454362236782846)
XLA Ops:
  8.0 74.8 %all-gather.2.cloned.1.call-done = bf16[1,2560,640]{2,1,0:T(8,128)(2,1)} async-done(((bf16[1,80,640]{2,1,0:T(8,128)(2,1)}), bf16[1,2560,640]{2,1,0:T(8,128)(2,1)}) %all-gather.2.cloned.1.call-update) | async-done | bytes 3276816 | tf_op jit(solution)/shard_map/all_gather | solution.py:66
  85.3 224.0 %while.37 = (s32[]{:T(128)}, bf16[64,640]{1,0:T(8,128)(2,1)S(1)}, bf16[256,640]{1,0:T(8,128)(2,1)}, f32[256,2560]{1,0:T(8,128)}, s32[]{:T(128)}, /*index=5*/pred...) while((s32[]{:T(128)}, bf16[64,640]{1,0:T(8,128)(2,1)S(1)}, ...), condition=%wide.region_4.5_spmd, body=%wide.region_0.4_spmd.sunk | while | flops 421068864 | bytes 22560664 | solution.py:135
  85.3 7.3 conditional.4
  87.9 4.0 multiply_reduce_fusion
  95.8 7.3 conditional.4
  98.4 4.0 multiply_reduce_fusion
  103.2 4.1 collective-permute-start
  108.8 7.3 conditional.4
  111.3 4.0 multiply_reduce_fusion
  116.1 3.7 collective-permute-start
  121.3 7.3 conditional.4
  123.8 4.0 multiply_reduce_fusion
  128.7 3.7 collective-permute-start
  133.9 11.0 %collective-permute-start = (bf16[64,640]{1,0:T(8,128)(2,1)S(1)}, bf16[64,640]{1,0:T(8,128)(2,1)S(1)}, u32[]{:S(2)}, u32[]{:S(2)}) collective-permute-start(bf16[64,640]{1,0:T(8,128)(2,1)S(1)} %get-tuple-element.806), channel_id=1, source_target_pairs={{0,32},{32,64},{64,96},{96,128},{128,160},{160,192},{192,224},{224... | collective-permute-start | bytes 245768 | tf_op jit(solution)/shard_map/while/body/eval_jaxpr/ppermute | solution.py:14
  146.4 3.7 collective-permute-start
  151.9 9.0 collective-permute-start
  162.4 6.1 collective-permute-start
  170.0 17.1 %collective-permute-start = (bf16[64,640]{1,0:T(8,128)(2,1)S(1)}, bf16[64,640]{1,0:T(8,128)(2,1)S(1)}, u32[]{:S(2)}, u32[]{:S(2)}) collective-permute-start(bf16[64,640]{1,0:T(8,128)(2,1)S(1)} %get-tuple-element.806), channel_id=1, source_target_pairs={{0,32},{32,64},{64,96},{96,128},{128,160},{160,192},{192,224},{224... | collective-permute-start | bytes 245768 | tf_op jit(solution)/shard_map/while/body/eval_jaxpr/ppermute | solution.py:14
  188.6 9.7 collective-permute-start
  199.8 17.1 %collective-permute-start = (bf16[64,640]{1,0:T(8,128)(2,1)S(1)}, bf16[64,640]{1,0:T(8,128)(2,1)S(1)}, u32[]{:S(2)}, u32[]{:S(2)}) collective-permute-start(bf16[64,640]{1,0:T(8,128)(2,1)S(1)} %get-tuple-element.806), channel_id=1, source_target_pairs={{0,32},{32,64},{64,96},{96,128},{128,160},{160,192},{192,224},{224... | collective-permute-start | bytes 245768 | tf_op jit(solution)/shard_map/while/body/eval_jaxpr/ppermute | solution.py:14
  218.4 9.7 collective-permute-start
  229.6 9.8 collective-permute-start
  241.5 9.9 collective-permute-start
  252.8 9.9 collective-permute-start
  264.2 9.6 collective-permute-start
  275.3 10.1 %collective-permute-start = (bf16[64,640]{1,0:T(8,128)(2,1)S(1)}, bf16[64,640]{1,0:T(8,128)(2,1)S(1)}, u32[]{:S(2)}, u32[]{:S(2)}) collective-permute-start(bf16[64,640]{1,0:T(8,128)(2,1)S(1)} %get-tuple-element.806), channel_id=1, source_target_pairs={{0,32},{32,64},{64,96},{96,128},{128,160},{160,192},{192,224},{224... | collective-permute-start | bytes 245768 | tf_op jit(solution)/shard_map/while/body/eval_jaxpr/ppermute | solution.py:14
  286.9 9.7 collective-permute-start
  298.1 9.7 collective-permute-start
  310.1 3.3 broadcast_in_dim.25
  313.4 475.2 %while.38 = (s32[]{:T(128)}, bf16[64,640]{1,0:T(8,128)(2,1)S(1)}, bf16[256,640]{1,0:T(8,128)(2,1)}, f32[2560,640]{1,0:T(8,128)}, s32[]{:T(128)}, /*index=5*/pred...) while((s32[]{:T(128)}, bf16[64,640]{1,0:T(8,128)(2,1)S(1)}, ...), condition=%wide.region_10.11_spmd, body=%wide.region_5.10_spmd.sunk | while | flops 846889024 | bytes 84667392 | solution.py:136
  314.7 10.3 %collective-permute-done.1 = bf16[64,640]{1,0:T(8,128)(2,1)S(1)} collective-permute-done((bf16[64,640]{1,0:T(8,128)(2,1)S(1)}, bf16[64,640]{1,0:T(8,128)(2,1)S(1)}, u32[]{:S(2)}, u32[]{:S(2)}) %collective-permute-start.1) | collective-permute-done | bytes 81952 | tf_op jit(solution)/shard_map/while/body/eval_jaxpr/ppermute | solution.py:14
  326.3 10.3 %collective-permute-done.1 = bf16[64,640]{1,0:T(8,128)(2,1)S(1)} collective-permute-done((bf16[64,640]{1,0:T(8,128)(2,1)S(1)}, bf16[64,640]{1,0:T(8,128)(2,1)S(1)}, u32[]{:S(2)}, u32[]{:S(2)}) %collective-permute-start.1) | collective-permute-done | bytes 81952 | tf_op jit(solution)/shard_map/while/body/eval_jaxpr/ppermute | solution.py:14
  337.9 10.3 %collective-permute-done.1 = bf16[64,640]{1,0:T(8,128)(2,1)S(1)} collective-permute-done((bf16[64,640]{1,0:T(8,128)(2,1)S(1)}, bf16[64,640]{1,0:T(8,128)(2,1)S(1)}, u32[]{:S(2)}, u32[]{:S(2)}) %collective-permute-start.1) | collective-permute-done | bytes 81952 | tf_op jit(solution)/shard_map/while/body/eval_jaxpr/ppermute | solution.py:14
  349.5 10.4 %collective-permute-done.1 = bf16[64,640]{1,0:T(8,128)(2,1)S(1)} collective-permute-done((bf16[64,640]{1,0:T(8,128)(2,1)S(1)}, bf16[64,640]{1,0:T(8,128)(2,1)S(1)}, u32[]{:S(2)}, u32[]{:S(2)}) %collective-permute-start.1) | collective-permute-done | bytes 81952 | tf_op jit(solution)/shard_map/while/body/eval_jaxpr/ppermute | solution.py:14
  361.2 10.2 %collective-permute-done.1 = bf16[64,640]{1,0:T(8,128)(2,1)S(1)} collective-permute-done((bf16[64,640]{1,0:T(8,128)(2,1)S(1)}, bf16[64,640]{1,0:T(8,128)(2,1)S(1)}, u32[]{:S(2)}, u32[]{:S(2)}) %collective-permute-start.1) | collective-permute-done | bytes 81952 | tf_op jit(solution)/shard_map/while/body/eval_jaxpr/ppermute | solution.py:14
  372.8 11.4 %collective-permute-done.1 = bf16[64,640]{1,0:T(8,128)(2,1)S(1)} collective-permute-done((bf16[64,640]{1,0:T(8,128)(2,1)S(1)}, bf16[64,640]{1,0:T(8,128)(2,1)S(1)}, u32[]{:S(2)}, u32[]{:S(2)}) %collective-permute-start.1) | collective-permute-done | bytes 81952 | tf_op jit(solution)/shard_map/while/body/eval_jaxpr/ppermute | solution.py:14
  385.5 10.4 %collective-permute-done.1 = bf16[64,640]{1,0:T(8,128)(2,1)S(1)} collective-permute-done((bf16[64,640]{1,0:T(8,128)(2,1)S(1)}, bf16[64,640]{1,0:T(8,128)(2,1)S(1)}, u32[]{:S(2)}, u32[]{:S(2)}) %collective-permute-start.1) | collective-permute-done | bytes 81952 | tf_op jit(solution)/shard_map/while/body/eval_jaxpr/ppermute | solution.py:14
  397.2 10.2 %collective-permute-done.1 = bf16[64,640]{1,0:T(8,128)(2,1)S(1)} collective-permute-done((bf16[64,640]{1,0:T(8,128)(2,1)S(1)}, bf16[64,640]{1,0:T(8,128)(2,1)S(1)}, u32[]{:S(2)}, u32[]{:S(2)}) %collective-permute-start.1) | collective-permute-done | bytes 81952 | tf_op jit(solution)/shard_map/while/body/eval_jaxpr/ppermute | solution.py:14
  408.7 10.8 %collective-permute-done.1 = bf16[64,640]{1,0:T(8,128)(2,1)S(1)} collective-permute-done((bf16[64,640]{1,0:T(8,128)(2,1)S(1)}, bf16[64,640]{1,0:T(8,128)(2,1)S(1)}, u32[]{:S(2)}, u32[]{:S(2)}) %collective-permute-start.1) | collective-permute-done | bytes 81952 | tf_op jit(solution)/shard_map/while/body/eval_jaxpr/ppermute | solution.py:14
  420.8 12.5 %collective-permute-done.1 = bf16[64,640]{1,0:T(8,128)(2,1)S(1)} collective-permute-done((bf16[64,640]{1,0:T(8,128)(2,1)S(1)}, bf16[64,640]{1,0:T(8,128)(2,1)S(1)}, u32[]{:S(2)}, u32[]{:S(2)}) %collective-permute-start.1) | collective-permute-done | bytes 81952 | tf_op jit(solution)/shard_map/while/body/eval_jaxpr/ppermute | solution.py:14
  434.7 10.7 %collective-permute-done.1 = bf16[64,640]{1,0:T(8,128)(2,1)S(1)} collective-permute-done((bf16[64,640]{1,0:T(8,128)(2,1)S(1)}, bf16[64,640]{1,0:T(8,128)(2,1)S(1)}, u32[]{:S(2)}, u32[]{:S(2)}) %collective-permute-start.1) | collective-permute-done | bytes 81952 | tf_op jit(solution)/shard_map/while/body/eval_jaxpr/ppermute | solution.py:14
  446.7 12.0 %collective-permute-done.1 = bf16[64,640]{1,0:T(8,128)(2,1)S(1)} collective-permute-done((bf16[64,640]{1,0:T(8,128)(2,1)S(1)}, bf16[64,640]{1,0:T(8,128)(2,1)S(1)}, u32[]{:S(2)}, u32[]{:S(2)}) %collective-permute-start.1) | collective-permute-done | bytes 81952 | tf_op jit(solution)/shard_map/while/body/eval_jaxpr/ppermute | solution.py:14
  460.0 10.9 %collective-permute-done.1 = bf16[64,640]{1,0:T(8,128)(2,1)S(1)} collective-permute-done((bf16[64,640]{1,0:T(8,128)(2,1)S(1)}, bf16[64,640]{1,0:T(8,128)(2,1)S(1)}, u32[]{:S(2)}, u32[]{:S(2)}) %collective-permute-start.1) | collective-permute-done | bytes 81952 | tf_op jit(solution)/shard_map/while/body/eval_jaxpr/ppermute | solution.py:14
  472.2 10.8 %collective-permute-done.1 = bf16[64,640]{1,0:T(8,128)(2,1)S(1)} collective-permute-done((bf16[64,640]{1,0:T(8,128)(2,1)S(1)}, bf16[64,640]{1,0:T(8,128)(2,1)S(1)}, u32[]{:S(2)}, u32[]{:S(2)}) %collective-permute-start.1) | collective-permute-done | bytes 81952 | tf_op jit(solution)/shard_map/while/body/eval_jaxpr/ppermute | solution.py:14
  484.4 195.4 %collective-permute-done.1 = bf16[64,640]{1,0:T(8,128)(2,1)S(1)} collective-permute-done((bf16[64,640]{1,0:T(8,128)(2,1)S(1)}, bf16[64,640]{1,0:T(8,128)(2,1)S(1)}, u32[]{:S(2)}, u32[]{:S(2)}) %collective-permute-start.1) | collective-permute-done | bytes 81952 | tf_op jit(solution)/shard_map/while/body/eval_jaxpr/ppermute | solution.py:14
  679.8 17.0 %conditional.5 = (bf16[256,640]{1,0:T(8,128)(2,1)}, f32[2560,640]{1,0:T(8,128)}, bf16[64,640]{1,0:T(8,128)(2,1)S(1)}) conditional(s32[]{:T(128)} %convert_element_type.73, (bf16[256,640]{1,0:T(8,128)(2,1)}, f32[2560,640]{1,0:T(8,128)}) %tuple.116, (pred[]{:T(512)}, s32[]{:T(128)}, bf16[256,640]{1,0:T(8,128)(2,1)}, bf16[64,640]{1,0:T(8,128)(2,1)S(1)}, ...), branch_computations={%region_6.6_spmd, %region_7.9_spmd} | conditional | flops 846889024 | bytes 84339408 | solution.py:114
  690.0 4.0 add_add_fusion
  694.0 2.7 copy-done.2
  698.0 9.9 %collective-permute-done.1 = bf16[64,640]{1,0:T(8,128)(2,1)S(1)} collective-permute-done((bf16[64,640]{1,0:T(8,128)(2,1)S(1)}, bf16[64,640]{1,0:T(8,128)(2,1)S(1)}, u32[]{:S(2)}, u32[]{:S(2)}) %collective-permute-start.1) | collective-permute-done | bytes 81952 | tf_op jit(solution)/shard_map/while/body/eval_jaxpr/ppermute | solution.py:14
  708.0 17.0 %conditional.5 = (bf16[256,640]{1,0:T(8,128)(2,1)}, f32[2560,640]{1,0:T(8,128)}, bf16[64,640]{1,0:T(8,128)(2,1)S(1)}) conditional(s32[]{:T(128)} %convert_element_type.73, (bf16[256,640]{1,0:T(8,128)(2,1)}, f32[2560,640]{1,0:T(8,128)}) %tuple.116, (pred[]{:T(512)}, s32[]{:T(128)}, bf16[256,640]{1,0:T(8,128)(2,1)}, bf16[64,640]{1,0:T(8,128)(2,1)S(1)}, ...), branch_computations={%region_6.6_spmd, %region_7.9_spmd} | conditional | flops 846889024 | bytes 84339408 | solution.py:114
  718.2 4.0 add_add_fusion
  722.2 2.7 copy-done.2
  726.2 10.8 %collective-permute-done.1 = bf16[64,640]{1,0:T(8,128)(2,1)S(1)} collective-permute-done((bf16[64,640]{1,0:T(8,128)(2,1)S(1)}, bf16[64,640]{1,0:T(8,128)(2,1)S(1)}, u32[]{:S(2)}, u32[]{:S(2)}) %collective-permute-start.1) | collective-permute-done | bytes 81952 | tf_op jit(solution)/shard_map/while/body/eval_jaxpr/ppermute | solution.py:14
  737.0 17.0 %conditional.5 = (bf16[256,640]{1,0:T(8,128)(2,1)}, f32[2560,640]{1,0:T(8,128)}, bf16[64,640]{1,0:T(8,128)(2,1)S(1)}) conditional(s32[]{:T(128)} %convert_element_type.73, (bf16[256,640]{1,0:T(8,128)(2,1)}, f32[2560,640]{1,0:T(8,128)}) %tuple.116, (pred[]{:T(512)}, s32[]{:T(128)}, bf16[256,640]{1,0:T(8,128)(2,1)}, bf16[64,640]{1,0:T(8,128)(2,1)S(1)}, ...), branch_computations={%region_6.6_spmd, %region_7.9_spmd} | conditional | flops 846889024 | bytes 84339408 | solution.py:114
  739.2 2.4 multiply_reduce_fusion.1
  747.2 4.0 add_add_fusion
  751.2 2.7 copy-done.2
  755.2 11.2 %collective-permute-done.1 = bf16[64,640]{1,0:T(8,128)(2,1)S(1)} collective-permute-done((bf16[64,640]{1,0:T(8,128)(2,1)S(1)}, bf16[64,640]{1,0:T(8,128)(2,1)S(1)}, u32[]{:S(2)}, u32[]{:S(2)}) %collective-permute-start.1) | collective-permute-done | bytes 81952 | tf_op jit(solution)/shard_map/while/body/eval_jaxpr/ppermute | solution.py:14
  766.5 17.0 %conditional.5 = (bf16[256,640]{1,0:T(8,128)(2,1)}, f32[2560,640]{1,0:T(8,128)}, bf16[64,640]{1,0:T(8,128)(2,1)S(1)}) conditional(s32[]{:T(128)} %convert_element_type.73, (bf16[256,640]{1,0:T(8,128)(2,1)}, f32[2560,640]{1,0:T(8,128)}) %tuple.116, (pred[]{:T(512)}, s32[]{:T(128)}, bf16[256,640]{1,0:T(8,128)(2,1)}, bf16[64,640]{1,0:T(8,128)(2,1)S(1)}, ...), branch_computations={%region_6.6_spmd, %region_7.9_spmd} | conditional | flops 846889024 | bytes 84339408 | solution.py:114
  776.7 4.0 add_add_fusion
  780.7 2.7 copy-done.2
  784.7 3.9 collective-permute-done.1
  788.6 5.0 convert_element_type.58
  793.6 188.1 %reduce-scatter.2.cloned.1.call-done = bf16[80,640]{1,0:T(8,128)(2,1)} async-done(((bf16[2560,640]{1,0:T(8,128)(2,1)}), bf16[80,640]{1,0:T(8,128)(2,1)}) %reduce-scatter.2.cloned.1.call-update) | async-done | bytes 102416 | tf_op jit(solution)/shard_map/reduce_scatter | solution.py:139
  (196 shorter events, 112.7 us)
Async XLA Ops:
  7.2 75.6 %all-gather.2.cloned.1.call-start = ((), (), s32[]{:S(2)}) async-start(), calls=%async_computation.1 | async-start | bytes 3379200 | tf_op jit(solution)/shard_map/all_gather | solution.py:66
  7.9 973.8 %reduce-scatter.2.cloned.1.call-start = ((), (), s32[]{:S(2)}) async-start(), calls=%async_computation.2 | async-start | bytes 3379200 | tf_op jit(solution)/shard_map/reduce_scatter | solution.py:139
  85.3 6.6 copy-start
  92.7 3.2 collective-permute-start
  95.8 6.6 copy-start
  103.2 5.6 collective-permute-start
  108.8 6.6 copy-start
  116.1 5.2 collective-permute-start
  121.3 6.6 copy-start
  128.7 5.2 collective-permute-start
  133.9 12.5 %collective-permute-start = (bf16[64,640]{1,0:T(8,128)(2,1)S(1)}, bf16[64,640]{1,0:T(8,128)(2,1)S(1)}, u32[]{:S(2)}, u32[]{:S(2)}) collective-permute-start(bf16[64,640]{1,0:T(8,128)(2,1)S(1)} %get-tuple-element.806), channel_id=1, source_target_pairs={{0,32},{32,64},{64,96},{96,128},{128,160},{160,192},{192,224},{224... | collective-permute-start | bytes 245768 | tf_op jit(solution)/shard_map/while/body/eval_jaxpr/ppermute | solution.py:14
  146.4 5.4 collective-permute-start
  151.9 10.5 %collective-permute-start = (bf16[64,640]{1,0:T(8,128)(2,1)S(1)}, bf16[64,640]{1,0:T(8,128)(2,1)S(1)}, u32[]{:S(2)}, u32[]{:S(2)}) collective-permute-start(bf16[64,640]{1,0:T(8,128)(2,1)S(1)} %get-tuple-element.806), channel_id=1, source_target_pairs={{0,32},{32,64},{64,96},{96,128},{128,160},{160,192},{192,224},{224... | collective-permute-start | bytes 245768 | tf_op jit(solution)/shard_map/while/body/eval_jaxpr/ppermute | solution.py:14
  162.4 7.6 collective-permute-start
  170.0 18.5 %collective-permute-start = (bf16[64,640]{1,0:T(8,128)(2,1)S(1)}, bf16[64,640]{1,0:T(8,128)(2,1)S(1)}, u32[]{:S(2)}, u32[]{:S(2)}) collective-permute-start(bf16[64,640]{1,0:T(8,128)(2,1)S(1)} %get-tuple-element.806), channel_id=1, source_target_pairs={{0,32},{32,64},{64,96},{96,128},{128,160},{160,192},{192,224},{224... | collective-permute-start | bytes 245768 | tf_op jit(solution)/shard_map/while/body/eval_jaxpr/ppermute | solution.py:14
  188.6 11.2 %collective-permute-start = (bf16[64,640]{1,0:T(8,128)(2,1)S(1)}, bf16[64,640]{1,0:T(8,128)(2,1)S(1)}, u32[]{:S(2)}, u32[]{:S(2)}) collective-permute-start(bf16[64,640]{1,0:T(8,128)(2,1)S(1)} %get-tuple-element.806), channel_id=1, source_target_pairs={{0,32},{32,64},{64,96},{96,128},{128,160},{160,192},{192,224},{224... | collective-permute-start | bytes 245768 | tf_op jit(solution)/shard_map/while/body/eval_jaxpr/ppermute | solution.py:14
  199.8 18.5 %collective-permute-start = (bf16[64,640]{1,0:T(8,128)(2,1)S(1)}, bf16[64,640]{1,0:T(8,128)(2,1)S(1)}, u32[]{:S(2)}, u32[]{:S(2)}) collective-permute-start(bf16[64,640]{1,0:T(8,128)(2,1)S(1)} %get-tuple-element.806), channel_id=1, source_target_pairs={{0,32},{32,64},{64,96},{96,128},{128,160},{160,192},{192,224},{224... | collective-permute-start | bytes 245768 | tf_op jit(solution)/shard_map/while/body/eval_jaxpr/ppermute | solution.py:14
  218.4 11.2 %collective-permute-start = (bf16[64,640]{1,0:T(8,128)(2,1)S(1)}, bf16[64,640]{1,0:T(8,128)(2,1)S(1)}, u32[]{:S(2)}, u32[]{:S(2)}) collective-permute-start(bf16[64,640]{1,0:T(8,128)(2,1)S(1)} %get-tuple-element.806), channel_id=1, source_target_pairs={{0,32},{32,64},{64,96},{96,128},{128,160},{160,192},{192,224},{224... | collective-permute-start | bytes 245768 | tf_op jit(solution)/shard_map/while/body/eval_jaxpr/ppermute | solution.py:14
  229.6 11.8 %collective-permute-start = (bf16[64,640]{1,0:T(8,128)(2,1)S(1)}, bf16[64,640]{1,0:T(8,128)(2,1)S(1)}, u32[]{:S(2)}, u32[]{:S(2)}) collective-permute-start(bf16[64,640]{1,0:T(8,128)(2,1)S(1)} %get-tuple-element.806), channel_id=1, source_target_pairs={{0,32},{32,64},{64,96},{96,128},{128,160},{160,192},{192,224},{224... | collective-permute-start | bytes 245768 | tf_op jit(solution)/shard_map/while/body/eval_jaxpr/ppermute | solution.py:14
  241.5 11.3 %collective-permute-start = (bf16[64,640]{1,0:T(8,128)(2,1)S(1)}, bf16[64,640]{1,0:T(8,128)(2,1)S(1)}, u32[]{:S(2)}, u32[]{:S(2)}) collective-permute-start(bf16[64,640]{1,0:T(8,128)(2,1)S(1)} %get-tuple-element.806), channel_id=1, source_target_pairs={{0,32},{32,64},{64,96},{96,128},{128,160},{160,192},{192,224},{224... | collective-permute-start | bytes 245768 | tf_op jit(solution)/shard_map/while/body/eval_jaxpr/ppermute | solution.py:14
  252.8 11.4 %collective-permute-start = (bf16[64,640]{1,0:T(8,128)(2,1)S(1)}, bf16[64,640]{1,0:T(8,128)(2,1)S(1)}, u32[]{:S(2)}, u32[]{:S(2)}) collective-permute-start(bf16[64,640]{1,0:T(8,128)(2,1)S(1)} %get-tuple-element.806), channel_id=1, source_target_pairs={{0,32},{32,64},{64,96},{96,128},{128,160},{160,192},{192,224},{224... | collective-permute-start | bytes 245768 | tf_op jit(solution)/shard_map/while/body/eval_jaxpr/ppermute | solution.py:14
  264.2 11.0 %collective-permute-start = (bf16[64,640]{1,0:T(8,128)(2,1)S(1)}, bf16[64,640]{1,0:T(8,128)(2,1)S(1)}, u32[]{:S(2)}, u32[]{:S(2)}) collective-permute-start(bf16[64,640]{1,0:T(8,128)(2,1)S(1)} %get-tuple-element.806), channel_id=1, source_target_pairs={{0,32},{32,64},{64,96},{96,128},{128,160},{160,192},{192,224},{224... | collective-permute-start | bytes 245768 | tf_op jit(solution)/shard_map/while/body/eval_jaxpr/ppermute | solution.py:14
  275.3 11.6 %collective-permute-start = (bf16[64,640]{1,0:T(8,128)(2,1)S(1)}, bf16[64,640]{1,0:T(8,128)(2,1)S(1)}, u32[]{:S(2)}, u32[]{:S(2)}) collective-permute-start(bf16[64,640]{1,0:T(8,128)(2,1)S(1)} %get-tuple-element.806), channel_id=1, source_target_pairs={{0,32},{32,64},{64,96},{96,128},{128,160},{160,192},{192,224},{224... | collective-permute-start | bytes 245768 | tf_op jit(solution)/shard_map/while/body/eval_jaxpr/ppermute | solution.py:14
  286.9 11.2 %collective-permute-start = (bf16[64,640]{1,0:T(8,128)(2,1)S(1)}, bf16[64,640]{1,0:T(8,128)(2,1)S(1)}, u32[]{:S(2)}, u32[]{:S(2)}) collective-permute-start(bf16[64,640]{1,0:T(8,128)(2,1)S(1)} %get-tuple-element.806), channel_id=1, source_target_pairs={{0,32},{32,64},{64,96},{96,128},{128,160},{160,192},{192,224},{224... | collective-permute-start | bytes 245768 | tf_op jit(solution)/shard_map/while/body/eval_jaxpr/ppermute | solution.py:14
  298.1 11.2 %collective-permute-start = (bf16[64,640]{1,0:T(8,128)(2,1)S(1)}, bf16[64,640]{1,0:T(8,128)(2,1)S(1)}, u32[]{:S(2)}, u32[]{:S(2)}) collective-permute-start(bf16[64,640]{1,0:T(8,128)(2,1)S(1)} %get-tuple-element.806), channel_id=1, source_target_pairs={{0,32},{32,64},{64,96},{96,128},{128,160},{160,192},{192,224},{224... | collective-permute-start | bytes 245768 | tf_op jit(solution)/shard_map/while/body/eval_jaxpr/ppermute | solution.py:14
  310.1 3.3 copy-start.1
  310.1 3.3 copy-start.3
  313.4 11.6 %collective-permute-start.1 = (bf16[64,640]{1,0:T(8,128)(2,1)S(1)}, bf16[64,640]{1,0:T(8,128)(2,1)S(1)}, u32[]{:S(2)}, u32[]{:S(2)}) collective-permute-start(bf16[64,640]{1,0:T(8,128)(2,1)S(1)} %get-tuple-element.820), channel_id=1, source_target_pairs={{32,0},{64,32},{96,64},{128,96},{160,128},{192,160},{224,192},{256... | collective-permute-start | bytes 245768 | tf_op jit(solution)/shard_map/while/body/eval_jaxpr/ppermute | solution.py:14
  325.0 11.6 %collective-permute-start.1 = (bf16[64,640]{1,0:T(8,128)(2,1)S(1)}, bf16[64,640]{1,0:T(8,128)(2,1)S(1)}, u32[]{:S(2)}, u32[]{:S(2)}) collective-permute-start(bf16[64,640]{1,0:T(8,128)(2,1)S(1)} %get-tuple-element.820), channel_id=1, source_target_pairs={{32,0},{64,32},{96,64},{128,96},{160,128},{192,160},{224,192},{256... | collective-permute-start | bytes 245768 | tf_op jit(solution)/shard_map/while/body/eval_jaxpr/ppermute | solution.py:14
  336.6 11.6 %collective-permute-start.1 = (bf16[64,640]{1,0:T(8,128)(2,1)S(1)}, bf16[64,640]{1,0:T(8,128)(2,1)S(1)}, u32[]{:S(2)}, u32[]{:S(2)}) collective-permute-start(bf16[64,640]{1,0:T(8,128)(2,1)S(1)} %get-tuple-element.820), channel_id=1, source_target_pairs={{32,0},{64,32},{96,64},{128,96},{160,128},{192,160},{224,192},{256... | collective-permute-start | bytes 245768 | tf_op jit(solution)/shard_map/while/body/eval_jaxpr/ppermute | solution.py:14
  348.2 11.7 %collective-permute-start.1 = (bf16[64,640]{1,0:T(8,128)(2,1)S(1)}, bf16[64,640]{1,0:T(8,128)(2,1)S(1)}, u32[]{:S(2)}, u32[]{:S(2)}) collective-permute-start(bf16[64,640]{1,0:T(8,128)(2,1)S(1)} %get-tuple-element.820), channel_id=1, source_target_pairs={{32,0},{64,32},{96,64},{128,96},{160,128},{192,160},{224,192},{256... | collective-permute-start | bytes 245768 | tf_op jit(solution)/shard_map/while/body/eval_jaxpr/ppermute | solution.py:14
  359.9 11.5 %collective-permute-start.1 = (bf16[64,640]{1,0:T(8,128)(2,1)S(1)}, bf16[64,640]{1,0:T(8,128)(2,1)S(1)}, u32[]{:S(2)}, u32[]{:S(2)}) collective-permute-start(bf16[64,640]{1,0:T(8,128)(2,1)S(1)} %get-tuple-element.820), channel_id=1, source_target_pairs={{32,0},{64,32},{96,64},{128,96},{160,128},{192,160},{224,192},{256... | collective-permute-start | bytes 245768 | tf_op jit(solution)/shard_map/while/body/eval_jaxpr/ppermute | solution.py:14
  371.5 12.7 %collective-permute-start.1 = (bf16[64,640]{1,0:T(8,128)(2,1)S(1)}, bf16[64,640]{1,0:T(8,128)(2,1)S(1)}, u32[]{:S(2)}, u32[]{:S(2)}) collective-permute-start(bf16[64,640]{1,0:T(8,128)(2,1)S(1)} %get-tuple-element.820), channel_id=1, source_target_pairs={{32,0},{64,32},{96,64},{128,96},{160,128},{192,160},{224,192},{256... | collective-permute-start | bytes 245768 | tf_op jit(solution)/shard_map/while/body/eval_jaxpr/ppermute | solution.py:14
  384.2 11.7 %collective-permute-start.1 = (bf16[64,640]{1,0:T(8,128)(2,1)S(1)}, bf16[64,640]{1,0:T(8,128)(2,1)S(1)}, u32[]{:S(2)}, u32[]{:S(2)}) collective-permute-start(bf16[64,640]{1,0:T(8,128)(2,1)S(1)} %get-tuple-element.820), channel_id=1, source_target_pairs={{32,0},{64,32},{96,64},{128,96},{160,128},{192,160},{224,192},{256... | collective-permute-start | bytes 245768 | tf_op jit(solution)/shard_map/while/body/eval_jaxpr/ppermute | solution.py:14
  395.9 11.5 %collective-permute-start.1 = (bf16[64,640]{1,0:T(8,128)(2,1)S(1)}, bf16[64,640]{1,0:T(8,128)(2,1)S(1)}, u32[]{:S(2)}, u32[]{:S(2)}) collective-permute-start(bf16[64,640]{1,0:T(8,128)(2,1)S(1)} %get-tuple-element.820), channel_id=1, source_target_pairs={{32,0},{64,32},{96,64},{128,96},{160,128},{192,160},{224,192},{256... | collective-permute-start | bytes 245768 | tf_op jit(solution)/shard_map/while/body/eval_jaxpr/ppermute | solution.py:14
  407.4 12.1 %collective-permute-start.1 = (bf16[64,640]{1,0:T(8,128)(2,1)S(1)}, bf16[64,640]{1,0:T(8,128)(2,1)S(1)}, u32[]{:S(2)}, u32[]{:S(2)}) collective-permute-start(bf16[64,640]{1,0:T(8,128)(2,1)S(1)} %get-tuple-element.820), channel_id=1, source_target_pairs={{32,0},{64,32},{96,64},{128,96},{160,128},{192,160},{224,192},{256... | collective-permute-start | bytes 245768 | tf_op jit(solution)/shard_map/while/body/eval_jaxpr/ppermute | solution.py:14
  419.5 13.8 %collective-permute-start.1 = (bf16[64,640]{1,0:T(8,128)(2,1)S(1)}, bf16[64,640]{1,0:T(8,128)(2,1)S(1)}, u32[]{:S(2)}, u32[]{:S(2)}) collective-permute-start(bf16[64,640]{1,0:T(8,128)(2,1)S(1)} %get-tuple-element.820), channel_id=1, source_target_pairs={{32,0},{64,32},{96,64},{128,96},{160,128},{192,160},{224,192},{256... | collective-permute-start | bytes 245768 | tf_op jit(solution)/shard_map/while/body/eval_jaxpr/ppermute | solution.py:14
  433.4 12.0 %collective-permute-start.1 = (bf16[64,640]{1,0:T(8,128)(2,1)S(1)}, bf16[64,640]{1,0:T(8,128)(2,1)S(1)}, u32[]{:S(2)}, u32[]{:S(2)}) collective-permute-start(bf16[64,640]{1,0:T(8,128)(2,1)S(1)} %get-tuple-element.820), channel_id=1, source_target_pairs={{32,0},{64,32},{96,64},{128,96},{160,128},{192,160},{224,192},{256... | collective-permute-start | bytes 245768 | tf_op jit(solution)/shard_map/while/body/eval_jaxpr/ppermute | solution.py:14
  445.4 13.3 %collective-permute-start.1 = (bf16[64,640]{1,0:T(8,128)(2,1)S(1)}, bf16[64,640]{1,0:T(8,128)(2,1)S(1)}, u32[]{:S(2)}, u32[]{:S(2)}) collective-permute-start(bf16[64,640]{1,0:T(8,128)(2,1)S(1)} %get-tuple-element.820), channel_id=1, source_target_pairs={{32,0},{64,32},{96,64},{128,96},{160,128},{192,160},{224,192},{256... | collective-permute-start | bytes 245768 | tf_op jit(solution)/shard_map/while/body/eval_jaxpr/ppermute | solution.py:14
  458.7 12.2 %collective-permute-start.1 = (bf16[64,640]{1,0:T(8,128)(2,1)S(1)}, bf16[64,640]{1,0:T(8,128)(2,1)S(1)}, u32[]{:S(2)}, u32[]{:S(2)}) collective-permute-start(bf16[64,640]{1,0:T(8,128)(2,1)S(1)} %get-tuple-element.820), channel_id=1, source_target_pairs={{32,0},{64,32},{96,64},{128,96},{160,128},{192,160},{224,192},{256... | collective-permute-start | bytes 245768 | tf_op jit(solution)/shard_map/while/body/eval_jaxpr/ppermute | solution.py:14
  470.9 12.1 %collective-permute-start.1 = (bf16[64,640]{1,0:T(8,128)(2,1)S(1)}, bf16[64,640]{1,0:T(8,128)(2,1)S(1)}, u32[]{:S(2)}, u32[]{:S(2)}) collective-permute-start(bf16[64,640]{1,0:T(8,128)(2,1)S(1)} %get-tuple-element.820), channel_id=1, source_target_pairs={{32,0},{64,32},{96,64},{128,96},{160,128},{192,160},{224,192},{256... | collective-permute-start | bytes 245768 | tf_op jit(solution)/shard_map/while/body/eval_jaxpr/ppermute | solution.py:14
  483.1 196.7 %collective-permute-start.1 = (bf16[64,640]{1,0:T(8,128)(2,1)S(1)}, bf16[64,640]{1,0:T(8,128)(2,1)S(1)}, u32[]{:S(2)}, u32[]{:S(2)}) collective-permute-start(bf16[64,640]{1,0:T(8,128)(2,1)S(1)} %get-tuple-element.820), channel_id=1, source_target_pairs={{32,0},{64,32},{96,64},{128,96},{160,128},{192,160},{224,192},{256... | collective-permute-start | bytes 245768 | tf_op jit(solution)/shard_map/while/body/eval_jaxpr/ppermute | solution.py:14
  687.0 2.2 slice-start
  687.0 3.0 slice-start.1
  694.0 2.7 copy-start.2
  696.8 11.2 %collective-permute-start.1 = (bf16[64,640]{1,0:T(8,128)(2,1)S(1)}, bf16[64,640]{1,0:T(8,128)(2,1)S(1)}, u32[]{:S(2)}, u32[]{:S(2)}) collective-permute-start(bf16[64,640]{1,0:T(8,128)(2,1)S(1)} %get-tuple-element.820), channel_id=1, source_target_pairs={{32,0},{64,32},{96,64},{128,96},{160,128},{192,160},{224,192},{256... | collective-permute-start | bytes 245768 | tf_op jit(solution)/shard_map/while/body/eval_jaxpr/ppermute | solution.py:14
  715.2 2.2 slice-start
  715.2 3.0 slice-start.1
  722.2 2.7 copy-start.2
  724.9 12.1 %collective-permute-start.1 = (bf16[64,640]{1,0:T(8,128)(2,1)S(1)}, bf16[64,640]{1,0:T(8,128)(2,1)S(1)}, u32[]{:S(2)}, u32[]{:S(2)}) collective-permute-start(bf16[64,640]{1,0:T(8,128)(2,1)S(1)} %get-tuple-element.820), channel_id=1, source_target_pairs={{32,0},{64,32},{96,64},{128,96},{160,128},{192,160},{224,192},{256... | collective-permute-start | bytes 245768 | tf_op jit(solution)/shard_map/while/body/eval_jaxpr/ppermute | solution.py:14
  744.2 2.2 slice-start
  744.2 3.0 slice-start.1
  751.2 2.7 copy-start.2
  754.0 12.5 %collective-permute-start.1 = (bf16[64,640]{1,0:T(8,128)(2,1)S(1)}, bf16[64,640]{1,0:T(8,128)(2,1)S(1)}, u32[]{:S(2)}, u32[]{:S(2)}) collective-permute-start(bf16[64,640]{1,0:T(8,128)(2,1)S(1)} %get-tuple-element.820), channel_id=1, source_target_pairs={{32,0},{64,32},{96,64},{128,96},{160,128},{192,160},{224,192},{256... | collective-permute-start | bytes 245768 | tf_op jit(solution)/shard_map/while/body/eval_jaxpr/ppermute | solution.py:14
  773.7 2.2 slice-start
  773.7 3.0 slice-start.1
  780.7 2.7 copy-start.2
  783.4 5.2 collective-permute-start.1
Sparse Core Ops, SparseCore 0:
  10.1 72.5 all-gather.1
  793.7 187.9 reduce-scatter.1
where the time goes:
time: 997 us; the launch traced here: 990 us
  waiting for transfers between devices  675 us (68%)
  starting transfers between devices  190 us (19%)
  matrix products  58.3 us (6%)
  other arithmetic  30.6 us (3%)
  local copies, waits for them, and re-layouts  21.4 us (2%)
  between operations  14.1 us (1%)
    ppermute x38, waiting for transfers between devices, from_behind(): return lax.ppermute(shard, axis, pairs)  411 us
    ppermute x38, starting transfers between devices, from_behind(): return lax.ppermute(shard, axis, pairs)  190 us
    reduce_scatter x1, waiting for transfers between devices, shards(): lax.psum_scatter(stores[3].astype(jnp.bfloat16), 'dp', scatter_dimension=...  188 us
    all_gather x1, waiting for transfers between devices, shards(): weight = lax.all_gather(weights, 'dp', axis=1, tiled=True)[0]  74.8 us
    dot_general x8, matrix products, outer_sum(): jnp.einsum('rh,rc->hc', left, right, preferred_element_type=jnp.float32)  24.4 us
  transfers between devices with their start and end apart: 40, of which 40 were waited for; matrix products, arithmetic and copies ran while one was open for 0% of the time, Pallas kernels for 0%

commit v1 on v0

v1 whole, which is shorter than its diff:
```python
import math

import jax
import jax.numpy as jnp
from jax import lax
from jax.experimental import pallas as pl
from jax.experimental.pallas import tpu as pltpu
from jax.sharding import PartitionSpec as P

MESH = pl.DeviceIdType.MESH
BF, F32 = jnp.bfloat16, jnp.float32
C, H, T = 640, 2560, 64
ROWS, LANES = 80, 128
PLANS = 5
BLOCKS = 128


def bits_of(s, zl, y, c):
    xu, yu = lax.div(s, 2), lax.div(y, 2)
    xv, yv = lax.rem(lax.rem(s, 2) + xu, 2), lax.rem(lax.rem(y, 2) + yu, 2)
    return [xu, yu, lax.rem(zl, 2), xv, yv], lax.div(zl, 2), c


def place(plan, s, zl, y, c):
    dims, zb, core = bits_of(s, zl, y, c)
    at = zb + 64 * core
    for i in range(5):
        at = at + dims[(plan + i) % 5] * (2 << i)
    return at


def kernel(b_ref, w_ref, gain_ref, cot_ref, wg_ref, sg_ref,
           g, r, w, gains, xh, dn, da, cg, c_in, c_out, g_in, g_out, x_send,
           ag_s, ag_r, rs_s, rs_r, gn_s, gn_r, hop_s, hop_r, sg_s, sg_r):
    sec, dp = lax.axis_index("section"), lax.axis_index("dp")
    j, x = lax.div(sec, 4), lax.rem(sec, 4)
    zl, y, c = lax.div(dp, 8), lax.rem(lax.div(dp, 2), 4), lax.rem(dp, 2)

    def device(j, x, zl, y, c):
        return (j * 4 + x, zl * 8 + y * 2 + c)

    def flip(v):
        return v + 1 - 2 * lax.rem(v, 2)

    partner = [
        device(j, 3 - x, zl, y, c),
        device(j, x, zl, 3 - y, c),
        device(j, x, flip(zl), y, c),
        device(j, flip(x), zl, y, c),
        device(j, x, zl, flip(y), c),
    ]
    zb_partner = device(j, x, lax.rem(zl + 2, 4), y, c)
    core_partner = device(j, x, zl, y, 1 - c)
    ahead = device(lax.rem(j + 1, 4), x, zl, y, c)
    behind = device(lax.rem(j + 3, 4), x, zl, y, c)
    beside = [device(j, lax.rem(x + i, 4), zl, y, c) for i in (1, 2, 3)]

    barrier = pltpu.get_barrier_semaphore()
    peers = partner + [zb_partner, core_partner, ahead, behind, beside[1]]
    for peer in peers:
        pl.semaphore_signal(barrier, inc=1, device_id=peer, device_id_type=MESH)

    mine = [place(p, x, zl, y, c) for p in range(PLANS)]
    for p in range(PLANS):
        g[p, mine[p]] = w_ref[0, :, p * LANES:(p + 1) * LANES]
    gains[x] = gain_ref[...]
    pl.semaphore_wait(barrier, len(peers))

    def remote(src, dst, send, recv, to):
        return pltpu.make_async_remote_copy(
            src_ref=src, dst_ref=dst, send_sem=send, recv_sem=recv, device_id=to, device_id_type=MESH
        )

    def span(p, step):
        n = 1 << step
        return pl.ds(lax.div(mine[p], n) * n, n)

    def target(p, step):
        if step == 0:
            return zb_partner
        if step == 6:
            return core_partner
        return partner[(p + step - 1) % 5]

    gain_copies = [
        remote(gains.at[x], gains.at[x], gn_s.at[i], gn_r.at[i], beside[i]) for i in range(3)
    ]
    started = []
    for step in range(7):
        copies = []
        for p in range(PLANS):
            part = g.at[p, span(p, step)]
            copies.append(remote(part, part, ag_s.at[step, p], ag_r.at[step, p], target(p, step)))
            copies[-1].start()
        if step == 0:
            for copy in gain_copies:
                copy.start()
        for copy in copies:
            copy.wait_recv()
        started += copies
    for copy in gain_copies:
        copy.wait()
    for copy in started:
        copy.wait_send()

    def repack(i, carry):
        s, k = lax.div(i, 32), lax.rem(i, 32)
        z_, y_, c_ = lax.div(k, 8), lax.rem(lax.div(k, 2), 4), lax.rem(k, 2)
        for p in range(PLANS):
            w[s, pl.ds(pl.multiple_of(k * ROWS, 16), ROWS), p * LANES:(p + 1) * LANES] = g[p, place(p, s, z_, y_, c_)]
        return carry

    lax.fori_loop(0, 4 * 32, repack, 0)

    first = hop = None
    fwd = remote(c_out, c_in, hop_s.at[0], hop_r.at[0], ahead)
    bwd = remote(g_out, g_in, hop_s.at[1], hop_r.at[1], behind)

    @pl.when(j == 0)
    def _():
        c_out[...] = b_ref[pl.ds(pl.multiple_of(x * T, T), T), :]

    @pl.when(j > 0)
    def _():
        fwd.wait_recv()
        c_out[...] = c_in[...]

    def forward(s, carry):
        block = c_out[...]
        cg[s, :T, :] = block
        pre = lax.dot_general(block, w[s], (((1,), (1,)), ((), ())), preferred_element_type=F32)
        inv = lax.rsqrt(jnp.mean(pre * pre, axis=1, keepdims=True) + 1e-05)
        hat = pre * inv
        gain = gains[s]
        normed = hat * gain
        sig = 1.0 / (1.0 + jnp.exp(-normed))
        act = (normed * sig).astype(BF)
        xh[s] = hat
        dn[s] = sig * (1.0 + normed * (1.0 - sig)) * gain * inv
        da[s, T:, :] = act
        c_out[...] = (block.astype(F32) + jnp.dot(act, w[s], preferred_element_type=F32)).astype(BF)
        return carry

    lax.fori_loop(0, 4, forward, 0)

    @pl.when(j < 3)
    def _():
        fwd.start()

    @pl.when(j == 3)
    def _():
        g_out[...] = cot_ref[pl.ds(pl.multiple_of(x * T, T), T), :]

    @pl.when(j < 3)
    def _():
        bwd.wait_recv()
        g_out[...] = g_in[...]

    def backward(i, carry):
        s = 3 - i
        grad = g_out[...]
        cg[s, T:, :] = grad
        e = lax.dot_general(grad, w[s], (((1,), (1,)), ((), ())), preferred_element_type=F32) * dn[s]
        hat = xh[s]
        dpre = (e - hat * jnp.mean(e * hat, axis=1, keepdims=True)).astype(BF)
        da[s, :T, :] = dpre
        grad_in = (grad.astype(F32) + jnp.dot(dpre, w[s], preferred_element_type=F32)).astype(BF)
        g_out[...] = grad_in
        x_send[s] = grad_in
        return carry

    lax.fori_loop(0, 4, backward, 0)

    @pl.when(j > 0)
    def _():
        bwd.start()

    rows = pl.ds(pl.multiple_of(x * T, T), T)
    sg_ref[0, rows, :] = x_send[x]
    sg_copies = [
        remote(x_send.at[lax.rem(x + i, 4)], sg_ref.at[0, rows], sg_s.at[i - 1], sg_r.at[i - 1], beside[i - 1])
        for i in (1, 2, 3)
    ]
    for copy in sg_copies:
        copy.start()

    def outer(i, carry):
        s, z_ = lax.div(i, 4), lax.rem(i, 4)
        left = da[s, :, pl.ds(pl.multiple_of(z_ * 640, 128), 640)]
        grad = lax.dot_general(left, cg[s], (((0,), (0,)), ((), ())), preferred_element_type=F32).astype(BF)
        for t in range(8):
            for p in range(PLANS):
                g[p, place(p, s, z_, t // 2, t % 2)] = grad[t * ROWS:(t + 1) * ROWS, p * LANES:(p + 1) * LANES]
        return carry

    lax.fori_loop(0, 16, outer, 0)

    started = []
    for step in (6, 5, 4, 3, 2, 1, 0):
        n = 1 << step
        copies = []
        for p in range(PLANS):
            keep = lax.div(mine[p], n) * n
            away = keep + n - 2 * n * lax.rem(lax.div(mine[p], n), 2)
            copies.append(remote(g.at[p, pl.ds(away, n)], r.at[p, pl.ds(n - 1, n)], rs_s.at[step, p], rs_r.at[step, p], target(p, step)))
            copies[-1].start()
        started += copies
        for p in range(PLANS):
            keep = lax.div(mine[p], n) * n
            copies[p].wait_recv()

            def add(i, carry, p=p, keep=keep, n=n):
                g[p, keep + i] = g[p, keep + i] + r[p, n - 1 + i]
                return carry

            lax.fori_loop(0, n, add, 0, unroll=min(n, 8))

    for p in range(PLANS):
        wg_ref[0, :, p * LANES:(p + 1) * LANES] = g[p, mine[p]].astype(F32) * (1.0 / math.sqrt(8192))
    for copy in started:
        copy.wait_send()
    for copy in sg_copies:
        copy.wait()

    @pl.when(j < 3)
    def _():
        fwd.wait_send()

    @pl.when(j > 0)
    def _():
        bwd.wait_send()


def shards(boundary_in, weights, gains, cotangent):
    vmem = pl.BlockSpec(memory_space=pltpu.VMEM)
    dma = pltpu.SemaphoreType.DMA
    return pl.pallas_call(
        kernel,
        out_shape=(
            jax.ShapeDtypeStruct((1, ROWS, C), F32),
            jax.ShapeDtypeStruct((1, 4 * T, C), BF),
        ),
        in_specs=[vmem] * 4,
        out_specs=(vmem, vmem),
        scratch_shapes=[
            pltpu.VMEM((PLANS, BLOCKS, ROWS, LANES), BF),
            pltpu.VMEM((PLANS, BLOCKS, ROWS, LANES), BF),
            pltpu.VMEM((4, H, C), BF),
            pltpu.VMEM((4, 1, H), F32),
            pltpu.VMEM((4, T, H), F32),
            pltpu.VMEM((4, T, H), F32),
            pltpu.VMEM((4, 2 * T, H), BF),
            pltpu.VMEM((4, 2 * T, C), BF),
            pltpu.VMEM((T, C), BF),
            pltpu.VMEM((T, C), BF),
            pltpu.VMEM((T, C), BF),
            pltpu.VMEM((T, C), BF),
            pltpu.VMEM((4, T, C), BF),
            dma((7, PLANS)),
            dma((7, PLANS)),
            dma((7, PLANS)),
            dma((7, PLANS)),
            dma((3,)),
            dma((3,)),
            dma((2,)),
            dma((2,)),
            dma((3,)),
            dma((3,)),
        ],
        compiler_params=pltpu.CompilerParams(
            collective_id=0, has_side_effects=True, vmem_limit_bytes=60 << 20
        ),
    )(boundary_in, weights, gains, cotangent)


def solution(mesh):
    return jax.shard_map(
        shards,
        mesh=mesh,
        in_specs=(P("dp", None), P("section", "dp", None), P("section", None), P("dp", None)),
        out_specs=(P("section", "dp", None), P("section", "dp", None)),
        check_vma=False,
    )
```

time: 997 us -> 239 us (0.24)
  waiting for transfers between devices: 675 us -> 0 us
  Pallas kernels: 0 us -> 235 us
  starting transfers between devices: 190 us -> 0 us
  matrix products: 58.3 us -> 0 us
  other arithmetic: 30.6 us -> 0 us
  local copies, waits for them, and re-layouts: 21.4 us -> 2.4 us
  between operations: 14.1 us -> 0.65 us
    ppermute x38 -> x0, waiting for transfers between devices: 411 us -> none  [from_behind(): return lax.ppermute(shard, axis, pairs)]
    pallas_call x0 -> x1, Pallas kernels: none -> 235 us  [shards(): pl.pallas_call(kernel, out_shape=(jax.ShapeDtypeStruct((1, ROWS, C), F32)...]
    ppermute x38 -> x0, starting transfers between devices: 190 us -> none  [from_behind(): return lax.ppermute(shard, axis, pairs)]
    reduce_scatter x1 -> x0, waiting for transfers between devices: 188 us -> none  [shards(): lax.psum_scatter(stores[3].astype(jnp.bfloat16), 'dp', scatter_dimension=...]
    all_gather x1 -> x0, waiting for transfers between devices: 74.8 us -> none  [shards(): weight = lax.all_gather(weights, 'dp', axis=1, tiled=True)[0]]
    dot_general x24 -> x0, matrix products: 58.3 us -> none  [the longest x8 24.4 us: outer_sum(): jnp.einsum('rh,rc->hc', left, right, preferred_element_type=jnp.float32)]
    cond x32 -> x0, local copies, waits for them, and re-layouts: 14.5 us -> none
    convert_element_type x5 -> x0, other arithmetic: 10.1 us -> none  [the longest x4 5.12 us: section_backward(): grad_pre = (inv_rms * (grad_normed - pre_norm * inv_rms * inv_rms * jnp.m...]
  transfers between devices with their start and end apart: 40 -> 0, of which waited for: 40 -> 0; matrix products, arithmetic and copies ran while one was open for 0% -> 0% of each run, Pallas kernels for 0% -> 0%
where the time goes in v1:
time: 239 us; the launch traced here: 238 us
  Pallas kernels  235 us (98%)
  local copies, waits for them, and re-layouts  2.4 us (1%)
    pallas_call x1, Pallas kernels, shards(): pl.pallas_call(kernel, out_shape=(jax.ShapeDtypeStruct((1, ROWS, C), F32)...  235 us

profile of v1, /device:TPU:1, one launch (start us, length us, event | category | flops | bytes accessed | tf_op | source)
XLA Modules:
  0.0 238.3 jit_solution(13811909920902920454)
XLA Ops:
  0.6 235.3 %shard_map.59 = (f32[1,80,640]{2,1,0:T(8,128)}, bf16[1,256,640]{2,1,0:T(8,128)(2,1)}) custom-call(bf16[256,640]{1,0:T(8,128)(2,1)} %b_ref.1, bf16[1,80,640]{2,1,0:T(8,128)(2,1)} %w_ref.1, f32[1,2560]{1,0:T(1,128)} %gain_ref.1, bf16[256,640]{1,0:T(8,128)(2,1)} %cot_ref.1), custom_call_target="tpu_custom_call" | custom-call | tf_op jit(solution)/shard_map/pallas_call | solution.py:237
  235.9 0.0 copy-start
  235.9 1.7 copy.8
  237.6 0.0 copy-done
  237.6 0.7 copy.9
Async XLA Ops:
  235.9 1.7 copy-start

commit v2 on v1

v2 whole, which is shorter than its diff:
```python
import math

import jax
import jax.numpy as jnp
from jax import lax
from jax.experimental import pallas as pl
from jax.experimental.pallas import tpu as pltpu
from jax.sharding import PartitionSpec as P

MESH = pl.DeviceIdType.MESH
BF, F32 = jnp.bfloat16, jnp.float32
C, H, T = 640, 2560, 64
ROWS, LANES = 80, 128
PLANS = 5
BLOCKS = 128
HALF = H // 2
STREAMS = (slice(0, 48), slice(48, 80))


def bits_of(s, zl, y, c):
    xu, yu = lax.div(s, 2), lax.div(y, 2)
    xv, yv = lax.rem(lax.rem(s, 2) + xu, 2), lax.rem(lax.rem(y, 2) + yu, 2)
    return [xu, yu, lax.rem(zl, 2), xv, yv], lax.div(zl, 2), c


def place(plan, s, zl, y, c):
    dims, zb, core = bits_of(s, zl, y, c)
    at = zb + 64 * core
    for i in range(5):
        at = at + dims[(plan + i) % 5] * (2 << i)
    return at


def kernel(b_ref, w_ref, gain_ref, cot_ref, wg_ref, sg_ref,
           g, r, w, wt, gains, xh, dn, acts, acts_o, dpre, dpre_o, cs, cs_o, gs, gs_o,
           c_in, c_out, g_in, g_out, x_send,
           ag_s, ag_r, co_s, co_r, rs_s, rs_r, gn_s, gn_r, hop_s, hop_r, sg_s, sg_r, ex_s, ex_r):
    sec, dp = lax.axis_index("section"), lax.axis_index("dp")
    j, x = lax.div(sec, 4), lax.rem(sec, 4)
    zl, y, c = lax.div(dp, 8), lax.rem(lax.div(dp, 2), 4), lax.rem(dp, 2)

    def device(j, x, zl, y, c):
        return (j * 4 + x, zl * 8 + y * 2 + c)

    def flip(v):
        return v + 1 - 2 * lax.rem(v, 2)

    partner = [
        device(j, 3 - x, zl, y, c),
        device(j, x, zl, 3 - y, c),
        device(j, x, flip(zl), y, c),
        device(j, flip(x), zl, y, c),
        device(j, x, zl, flip(y), c),
    ]
    zb_partner = device(j, x, lax.rem(zl + 2, 4), y, c)
    core_partner = device(j, x, zl, y, 1 - c)
    ahead = device(lax.rem(j + 1, 4), x, zl, y, c)
    behind = device(lax.rem(j + 3, 4), x, zl, y, c)
    beside = [device(j, lax.rem(x + i, 4), zl, y, c) for i in (1, 2, 3)]

    barrier = pltpu.get_barrier_semaphore()
    peers = partner + [zb_partner, core_partner, ahead, behind, beside[1]]
    for peer in peers:
        pl.semaphore_signal(barrier, inc=1, device_id=peer, device_id_type=MESH)

    mine = [place(p, x, zl, y, c) for p in range(PLANS)]
    for p in range(PLANS):
        g[p, mine[p]] = w_ref[0, :, p * LANES:(p + 1) * LANES]
    gains[x] = jnp.concatenate(
        [gain_ref[:, (2 * i + h) * ROWS:(2 * i + h + 1) * ROWS] for h in (0, 1) for i in range(16)], axis=1
    )
    pl.semaphore_wait(barrier, len(peers))

    def remote(src, dst, send, recv, to):
        return pltpu.make_async_remote_copy(
            src_ref=src, dst_ref=dst, send_sem=send, recv_sem=recv, device_id=to, device_id_type=MESH
        )

    def target(p, step):
        return zb_partner if step == 0 else partner[(p + step - 1) % 5]

    def held(p, step):
        n = 1 << step
        return lax.div(mine[p], n) * n

    def other(p, step):
        n = 1 << step
        return held(p, step) + n - 2 * n * lax.rem(lax.div(mine[p], n), 2)

    def gather(p, step, h):
        part = g.at[p, pl.ds(held(p, step), 1 << step), STREAMS[h]]
        return remote(part, part, ag_s.at[step, p, h], ag_r.at[step, p, h], target(p, step))

    def across(p, late, h):
        part = g.at[p, pl.ds(other(p, 5) if late else held(p, 5), 32), STREAMS[h]]
        return remote(part, part, co_s.at[late, p, h], co_r.at[late, p, h], core_partner)

    gain_copies = [
        remote(gains.at[x], gains.at[x], gn_s.at[i], gn_r.at[i], beside[i]) for i in range(3)
    ]
    every = [(h, p) for h in range(2) for p in range(PLANS)]
    for h, p in every:
        gather(p, 0, h).start()
    for copy in gain_copies:
        copy.start()
    for step in range(1, 6):
        for h, p in every:
            gather(p, step - 1, h).wait_recv()
            gather(p, step, h).start()
    for h, p in every:
        across(p, 0, h).start()
    for h, p in every:
        gather(p, 5, h).wait_recv()
        across(p, 1, h).start()
    for copy in gain_copies:
        copy.wait()
    for h, p in every:
        across(p, 0, h).wait_recv()
        across(p, 1, h).wait_recv()

    def repack(i, carry):
        s, k = lax.div(i, 32), lax.rem(i, 32)
        c_, z_, y_ = lax.div(k, 16), lax.rem(lax.div(k, 4), 4), lax.rem(k, 4)
        for p in range(PLANS):
            w[s, pl.ds(pl.multiple_of(k * ROWS, 16), ROWS), p * LANES:(p + 1) * LANES] = g[p, place(p, s, z_, y_, c_)]
        return carry

    lax.fori_loop(0, 4 * 32, repack, 0)

    def transpose(i, carry):
        s, k = lax.div(i, 10), lax.rem(i, 10)
        at = pl.ds(pl.multiple_of(k * 256, 256), 256)
        wt[s, :, at] = w[s, at, :].T
        return carry

    fwd = remote(c_out, c_in, hop_s.at[0], hop_r.at[0], ahead)
    bwd = remote(g_out, g_in, hop_s.at[1], hop_r.at[1], behind)

    def forward(s, carry, ready=True):
        block = c_out[...]
        cs[s] = block
        if ready:
            pre = jnp.dot(block, wt[s], preferred_element_type=F32)
        else:
            pre = lax.dot_general(block, w[s], (((1,), (1,)), ((), ())), preferred_element_type=F32)
        inv = lax.rsqrt(jnp.mean(pre * pre, axis=1, keepdims=True) + 1e-05)
        hat = pre * inv
        gain = gains[s]
        normed = hat * gain
        sig = 1.0 / (1.0 + jnp.exp(-normed))
        act = (normed * sig).astype(BF)
        c_out[...] = (block.astype(F32) + jnp.dot(act, w[s], preferred_element_type=F32)).astype(BF)
        xh[s] = hat
        dn[s] = sig * (1.0 + normed * (1.0 - sig)) * gain * inv
        acts[s, 0] = act[:, :HALF]
        acts[s, 1] = act[:, HALF:]
        return carry

    @pl.when(j == 0)
    def _():
        c_out[...] = b_ref[pl.ds(pl.multiple_of(x * T, T), T), :]
        lax.fori_loop(0, 4, lambda s, carry: forward(s, carry, ready=False), 0)
        fwd.start()
        lax.fori_loop(0, 40, transpose, 0)

    @pl.when(j > 0)
    def _():
        lax.fori_loop(0, 40, transpose, 0)
        fwd.wait_recv()
        c_out[...] = c_in[...]
        lax.fori_loop(0, 4, forward, 0)

    @pl.when((j > 0) & (j < 3))
    def _():
        fwd.start()

    ex = [
        remote(acts.at[:, 1 - c], acts_o, ex_s.at[0], ex_r.at[0], core_partner),
        remote(cs, cs_o, ex_s.at[1], ex_r.at[1], core_partner),
    ]

    @pl.when(j < 3)
    def _():
        ex[0].start()
        ex[1].start()

    for h, p in every:
        for step in range(6):
            gather(p, step, h).wait_send()
        across(p, 0, h).wait_send()
        across(p, 1, h).wait_send()

    @pl.when(j == 3)
    def _():
        g_out[...] = cot_ref[pl.ds(pl.multiple_of(x * T, T), T), :]

    @pl.when(j < 3)
    def _():
        bwd.wait_recv()
        g_out[...] = g_in[...]

    def ex_dpre(s):
        return remote(dpre.at[s, 1 - c], dpre_o.at[s], ex_s.at[2 + s], ex_r.at[2 + s], core_partner)

    def ex_grad(s):
        return remote(gs.at[s], gs_o.at[s], ex_s.at[6 + s], ex_r.at[6 + s], core_partner)

    def backward(i, carry):
        s = 3 - i
        grad = g_out[...]
        gs[s] = grad
        ex_grad(s).start()
        e = jnp.dot(grad, wt[s], preferred_element_type=F32) * dn[s]
        hat = xh[s]
        dp = (e - hat * jnp.mean(e * hat, axis=1, keepdims=True)).astype(BF)
        dpre[s, 0] = dp[:, :HALF]
        dpre[s, 1] = dp[:, HALF:]
        ex_dpre(s).start()
        grad_in = (grad.astype(F32) + jnp.dot(dp, w[s], preferred_element_type=F32)).astype(BF)
        g_out[...] = grad_in
        x_send[s] = grad_in
        return carry

    lax.fori_loop(0, 4, backward, 0)

    @pl.when(j > 0)
    def _():
        bwd.start()

    @pl.when(j == 3)
    def _():
        ex[0].start()
        ex[1].start()

    rows = pl.ds(pl.multiple_of(x * T, T), T)
    sg_ref[0, rows, :] = x_send[x]
    sg_copies = [
        remote(x_send.at[lax.rem(x + i, 4)], sg_ref.at[0, rows], sg_s.at[i - 1], sg_r.at[i - 1], beside[i - 1])
        for i in (1, 2, 3)
    ]
    for copy in sg_copies:
        copy.start()

    ex[0].wait_recv()
    ex[1].wait_recv()

    def outer(i, carry):
        s = 3 - i
        ex_grad(s).wait_recv()
        ex_dpre(s).wait_recv()
        right = jnp.concatenate([cs[s], cs_o[s], gs[s], gs_o[s]], axis=0)
        for zh in range(2):
            at = slice(zh * 640, zh * 640 + 640)
            left = jnp.concatenate(
                [dpre[s, c, :, at], dpre_o[s, :, at], acts[s, c, :, at], acts_o[s, :, at]], axis=0
            )
            grad = lax.dot_general(left, right, (((0,), (0,)), ((), ())), preferred_element_type=F32).astype(BF)
            for t in range(8):
                for p in range(PLANS):
                    g[p, place(p, s, 2 * zh + t // 4, t % 4, 0)] = grad[t * ROWS:(t + 1) * ROWS, p * LANES:(p + 1) * LANES]
        return carry

    lax.fori_loop(0, 4, outer, 0)

    own = [m - 64 * c for m in mine]

    def first(p, step):
        n = 1 << step
        return lax.div(own[p], n) * n

    def second(p, step):
        n = 1 << step
        return first(p, step) + n - 2 * n * lax.rem(lax.div(own[p], n), 2)

    def reduce(p, step, h):
        n = 1 << step
        return remote(
            g.at[p, pl.ds(second(p, step), n), STREAMS[h]],
            r.at[p, pl.ds(n - 1, n), STREAMS[h]],
            rs_s.at[step, p, h], rs_r.at[step, p, h], target(p, step),
        )

    for h, p in every:
        reduce(p, 5, h).start()
    for step in range(5, -1, -1):
        for h, p in every:
            n = 1 << step
            base = first(p, step)
            reduce(p, step, h).wait_recv()

            def add(start, count, p=p, h=h, n=n, base=base):
                def one(i, carry):
                    at = start + i
                    g[p, at, STREAMS[h]] = g[p, at, STREAMS[h]] + r[p, n - 1 + at - base, STREAMS[h]]
                    return carry

                lax.fori_loop(0, count, one, 0, unroll=min(count, 8))

            if step:
                add(second(p, step - 1), n // 2)
                reduce(p, step - 1, h).start()
                add(first(p, step - 1), n // 2)
            else:
                add(base, 1)

    for p in range(PLANS):
        wg_ref[0, :, p * LANES:(p + 1) * LANES] = g[p, own[p]].astype(F32) * (1.0 / math.sqrt(8192))

    for h, p in every:
        for step in range(6):
            reduce(p, step, h).wait_send()
    for copy in sg_copies:
        copy.wait()
    ex[0].wait_send()
    ex[1].wait_send()

    def sent(s, carry):
        ex_grad(s).wait_send()
        ex_dpre(s).wait_send()
        return carry

    lax.fori_loop(0, 4, sent, 0)

    @pl.when(j < 3)
    def _():
        fwd.wait_send()

    @pl.when(j > 0)
    def _():
        bwd.wait_send()


def shards(boundary_in, weights, gains, cotangent):
    vmem = pl.BlockSpec(memory_space=pltpu.VMEM)
    dma = pltpu.SemaphoreType.DMA
    return pl.pallas_call(
        kernel,
        out_shape=(
            jax.ShapeDtypeStruct((1, ROWS, C), F32),
            jax.ShapeDtypeStruct((1, 4 * T, C), BF),
        ),
        in_specs=[vmem] * 4,
        out_specs=(vmem, vmem),
        scratch_shapes=[
            pltpu.VMEM((PLANS, BLOCKS, ROWS, LANES), BF),
            pltpu.VMEM((PLANS, BLOCKS // 2 - 1, ROWS, LANES), BF),
            pltpu.VMEM((4, H, C), BF),
            pltpu.VMEM((4, C, H), BF),
            pltpu.VMEM((4, 1, H), F32),
            pltpu.VMEM((4, T, H), F32),
            pltpu.VMEM((4, T, H), F32),
            pltpu.VMEM((4, 2, T, HALF), BF),
            pltpu.VMEM((4, T, HALF), BF),
            pltpu.VMEM((4, 2, T, HALF), BF),
            pltpu.VMEM((4, T, HALF), BF),
            pltpu.VMEM((4, T, C), BF),
            pltpu.VMEM((4, T, C), BF),
            pltpu.VMEM((4, T, C), BF),
            pltpu.VMEM((4, T, C), BF),
            pltpu.VMEM((T, C), BF),
            pltpu.VMEM((T, C), BF),
            pltpu.VMEM((T, C), BF),
            pltpu.VMEM((T, C), BF),
            pltpu.VMEM((4, T, C), BF),
            dma((6, PLANS, 2)),
            dma((6, PLANS, 2)),
            dma((2, PLANS, 2)),
            dma((2, PLANS, 2)),
            dma((6, PLANS, 2)),
            dma((6, PLANS, 2)),
            dma((3,)),
            dma((3,)),
            dma((2,)),
            dma((2,)),
            dma((3,)),
            dma((3,)),
            dma((10,)),
            dma((10,)),
        ],
        compiler_params=pltpu.CompilerParams(
            collective_id=0, has_side_effects=True, vmem_limit_bytes=60 << 20
        ),
    )(boundary_in, weights, gains, cotangent)


def solution(mesh):
    return jax.shard_map(
        shards,
        mesh=mesh,
        in_specs=(P("dp", None), P("section", "dp", None), P("section", None), P("dp", None)),
        out_specs=(P("section", "dp", None), P("section", "dp", None)),
        check_vma=False,
    )
```

time: 239 us -> 199 us (0.83); the launches traced: 238 us -> 196 us
  Pallas kernels: 235 us -> 193 us
    pallas_call x1, Pallas kernels: 235 us -> 193 us  [shards(): pl.pallas_call(kernel, out_shape=(jax.ShapeDtypeStruct((1, ROWS, C), F32)...]
where the time goes in v2:
time: 199 us; the launch traced here: 196 us
  Pallas kernels  193 us (97%)
  local copies, waits for them, and re-layouts  2.4 us (1%)
    pallas_call x1, Pallas kernels, shards(): pl.pallas_call(kernel, out_shape=(jax.ShapeDtypeStruct((1, ROWS, C), F32)...  193 us

profile of v2, /device:TPU:1, one launch (start us, length us, event | category | flops | bytes accessed | tf_op | source)
XLA Modules:
  0.0 195.6 jit_solution(8012672370784714121)
XLA Ops:
  0.6 192.5 %shard_map.59 = (f32[1,80,640]{2,1,0:T(8,128)}, bf16[1,256,640]{2,1,0:T(8,128)(2,1)}) custom-call(bf16[256,640]{1,0:T(8,128)(2,1)} %b_ref.1, bf16[1,80,640]{2,1,0:T(8,128)(2,1)} %w_ref.1, f32[1,2560]{1,0:T(1,128)} %gain_ref.1, bf16[256,640]{1,0:T(8,128)(2,1)} %cot_ref.1), custom_call_target="tpu_custom_call" | custom-call | tf_op jit(solution)/shard_map/pallas_call | solution.py:336
  193.2 0.0 copy-start
  193.2 1.7 copy.8
  194.9 0.0 copy-done
  194.9 0.7 copy.9
Async XLA Ops:
  193.2 1.7 copy-start

commit v3 on v2

v3 whole, which is shorter than its diff:
```python
import math

import jax
import jax.numpy as jnp
from jax import lax
from jax.experimental import pallas as pl
from jax.experimental.pallas import tpu as pltpu
from jax.sharding import PartitionSpec as P

MESH = pl.DeviceIdType.MESH
BF, F32 = jnp.bfloat16, jnp.float32
C, H, T = 640, 2560, 64
ROWS, LANES = 80, 128
PLANS = 5
BLOCKS = 128
HALF = H // 2
STREAMS = (slice(0, 48), slice(48, 80))
UNITS = [(h, p) for h in range(2) for p in range(PLANS)]

_FOUR, _ONE = ["xu", "yu", "za", "xv", "yv"], ["yu", "za", "yv"]
_TURN = [[0, 0], [1, 1], [2, 2], [0, 2], [1, 2]]
FOUR = [[["zb"] + [_FOUR[(p + i) % 5] for i in range(5)] for h in range(2)] for p in range(PLANS)]
ONE = [[["zb"] + [_ONE[(_TURN[p][h] + i) % 3] for i in range(3)] for h in range(2)] for p in range(PLANS)]


def place(order, s, zl, y, c):
    xu, yu = lax.div(s, 2), lax.div(y, 2)
    bits = {
        "xu": xu, "xv": lax.rem(lax.rem(s, 2) + xu, 2),
        "yu": yu, "yv": lax.rem(lax.rem(y, 2) + yu, 2),
        "za": lax.rem(zl, 2), "zb": lax.div(zl, 2),
    }
    at = c * (1 << len(order))
    for i, name in enumerate(order):
        at = at + bits[name] * (1 << i)
    return at


def kernel(b_ref, w_ref, gain_ref, cot_ref, wg_ref, sg_ref,
           g, r, w, wt, gains, xh, dn, acts, acts_o, dpre, dpre_o, cs, cs_o, gs, gs_o,
           c_in, c_out, g_in, g_out, x_send, x_back,
           ag_s, ag_r, co_s, co_r, rs_s, rs_r, gn_s, gn_r, hop_s, hop_r, sg_s, sg_r, ex_s, ex_r,
           up_s, up_r, down_s, down_r, relay_s, relay_r):
    sec, dp = lax.axis_index("section"), lax.axis_index("dp")
    j, x = lax.div(sec, 4), lax.rem(sec, 4)
    zl, y, c = lax.div(dp, 8), lax.rem(lax.div(dp, 2), 4), lax.rem(dp, 2)

    def device(j, x, zl, y, c):
        return (j * 4 + x, zl * 8 + y * 2 + c)

    def flip(v):
        return v + 1 - 2 * lax.rem(v, 2)

    partner = {
        "xu": device(j, 3 - x, zl, y, c),
        "xv": device(j, flip(x), zl, y, c),
        "yu": device(j, x, zl, 3 - y, c),
        "yv": device(j, x, zl, flip(y), c),
        "za": device(j, x, flip(zl), y, c),
        "zb": device(j, x, lax.rem(zl + 2, 4), y, c),
    }
    core_partner = device(j, x, zl, y, 1 - c)
    ahead = device(lax.rem(j + 1, 4), x, zl, y, c)
    behind = device(lax.rem(j + 3, 4), x, zl, y, c)
    beside = [device(j, lax.rem(x + i, 4), zl, y, c) for i in (1, 2, 3)]

    barrier = pltpu.get_barrier_semaphore()
    peers = list(partner.values()) + [core_partner, beside[1]]

    def greet(peer):
        pl.semaphore_signal(barrier, inc=1, device_id=peer, device_id_type=MESH)

    for peer in peers:
        greet(peer)

    def own_shard(orders, s):
        for h, p in UNITS:
            g[p, place(orders[p][h], s, zl, y, c), STREAMS[h]] = w_ref[0, STREAMS[h], p * LANES:(p + 1) * LANES]
        gains[s] = jnp.concatenate(
            [gain_ref[:, (2 * i + h) * ROWS:(2 * i + h + 1) * ROWS] for h in (0, 1) for i in range(16)], axis=1
        )

    last = device(0, 3, zl, y, c)

    @pl.when(j == 0)
    def _():
        own_shard(ONE, 0)
        pl.semaphore_wait(barrier, len(peers))

        @pl.when(x == 3)
        def _():
            for m in range(3):
                greet(device(1, m, zl, y, c))

    @pl.when(j > 0)
    def _():
        own_shard(FOUR, x)

        @pl.when((j == 1) & (x < 3))
        def _():
            pl.semaphore_wait(barrier, len(peers) + 2)

        @pl.when((j > 1) | (x == 3))
        def _():
            pl.semaphore_wait(barrier, len(peers) + 1)

        greet(behind)

    @pl.when(j < 3)
    def _():
        greet(ahead)

    def remote(src, dst, send, recv, to):
        return pltpu.make_async_remote_copy(
            src_ref=src, dst_ref=dst, send_sem=send, recv_sem=recv, device_id=to, device_id_type=MESH
        )

    def held(at, step):
        n = 1 << step
        return lax.div(at, n) * n

    def other(at, step):
        n = 1 << step
        return held(at, step) + n - 2 * n * lax.rem(lax.div(at, n), 2)

    def gathering(orders, s):
        steps = len(orders[0][0])

        def own(h, p):
            return place(orders[p][h], s, zl, y, c)

        def gather(h, p, step):
            part = g.at[p, pl.ds(held(own(h, p), step), 1 << step), STREAMS[h]]
            return remote(part, part, ag_s.at[step, p, h], ag_r.at[step, p, h], partner[orders[p][h][step]])

        def across(h, p, late):
            first = (other if late else held)(own(h, p), steps - 1)
            part = g.at[p, pl.ds(first, 1 << (steps - 1)), STREAMS[h]]
            return remote(part, part, co_s.at[late, p, h], co_r.at[late, p, h], core_partner)

        for unit in UNITS:
            gather(*unit, 0).start()
        for step in range(1, steps):
            for unit in UNITS:
                gather(*unit, step - 1).wait_recv()
                gather(*unit, step).start()
        for unit in UNITS:
            across(*unit, 0).start()
        for unit in UNITS:
            gather(*unit, steps - 1).wait_recv()
            across(*unit, 1).start()
        for unit in UNITS:
            across(*unit, 0).wait_recv()
            across(*unit, 1).wait_recv()

        def sends_done():
            for unit in UNITS:
                for step in range(steps):
                    gather(*unit, step).wait_send()
                across(*unit, 0).wait_send()
                across(*unit, 1).wait_send()

        return sends_done

    gain_copies = [
        remote(gains.at[x], gains.at[x], gn_s.at[i], gn_r.at[i], beside[i]) for i in range(3)
    ]

    def repack_four(i, carry):
        s, k = lax.div(i, 32), lax.rem(i, 32)
        c_, z_, y_ = lax.div(k, 16), lax.rem(lax.div(k, 4), 4), lax.rem(k, 4)
        for p in range(PLANS):
            at = place(FOUR[p][0], s, z_, y_, c_)
            w[s, pl.ds(pl.multiple_of(k * ROWS, 16), ROWS), p * LANES:(p + 1) * LANES] = g[p, at]
        return carry

    def repack_one(k, carry):
        c_, z_, y_ = lax.div(k, 16), lax.rem(lax.div(k, 4), 4), lax.rem(k, 4)
        for h, p in UNITS:
            rows = STREAMS[h]
            at = place(ONE[p][h], x, z_, y_, c_)
            to = pl.ds(pl.multiple_of(k * ROWS + rows.start, 16), rows.stop - rows.start)
            w[0, to, p * LANES:(p + 1) * LANES] = g[p, at, rows]
        return carry

    def transpose(i, carry):
        s, k = lax.div(i, 10), lax.rem(i, 10)
        at = pl.ds(pl.multiple_of(k * 256, 256), 256)
        wt[s, :, at] = w[s, at, :].T
        return carry

    fwd = remote(c_out, c_in, hop_s.at[0], hop_r.at[0], ahead)
    bwd = remote(g_out, g_in, hop_s.at[1], hop_r.at[1], behind)
    bwd_last = remote(g_out, gs.at[x], hop_s.at[1], down_r.at[x], last)

    def up(m):
        return remote(x_send.at[m], cs.at[m], up_s.at[m], up_r.at[m], device(j, lax.rem(x + 1, 4), zl, y, c))

    def down(m):
        return remote(x_back.at[m], gs.at[m], down_s.at[m], down_r.at[m], device(j, lax.rem(x + 3, 4), zl, y, c))

    def relay(m):
        return remote(x_send.at[m], c_in, relay_s.at[m], relay_r.at[0], device(j, m, zl, y, c))

    def forward(i, s, ready=True):
        block = cs[i]
        if ready:
            pre = jnp.dot(block, wt[s], preferred_element_type=F32)
        else:
            pre = lax.dot_general(block, w[s], (((1,), (1,)), ((), ())), preferred_element_type=F32)
        inv = lax.rsqrt(jnp.mean(pre * pre, axis=1, keepdims=True) + 1e-05)
        hat = pre * inv
        gain = gains[s]
        normed = hat * gain
        sig = 1.0 / (1.0 + jnp.exp(-normed))
        act = (normed * sig).astype(BF)
        xh[i] = hat
        dn[i] = sig * (1.0 + normed * (1.0 - sig)) * gain * inv
        acts[i, 0] = act[:, :HALF]
        acts[i, 1] = act[:, HALF:]
        return (block.astype(F32) + jnp.dot(act, w[s], preferred_element_type=F32)).astype(BF)

    @pl.when(j == 0)
    def _():
        sends_done = gathering(ONE, x)
        lax.fori_loop(0, 32, repack_one, 0)
        lax.fori_loop(0, 10, transpose, 0)

        @pl.when(x == 0)
        def _():
            for m in range(4):
                cs[m] = b_ref[m * T:(m + 1) * T, :]

        def step(m, carry):
            @pl.when(x > 0)
            def _():
                up(m).wait_recv()

            x_send[m] = forward(m, 0)

            @pl.when(x < 3)
            def _():
                up(m).start()

            @pl.when((x == 3) & (m < 3))
            def _():
                relay(m).start()

            return carry

        lax.fori_loop(0, 4, step, 0)

        @pl.when(x == 3)
        def _():
            c_out[...] = x_send[3]

        @pl.when(x < 3)
        def _():
            relay(0).wait_recv()
            c_out[...] = c_in[...]

        pl.semaphore_wait(barrier, 1)
        fwd.start()
        sends_done()

    @pl.when(j > 0)
    def _():
        for copy in gain_copies:
            copy.start()
        sends_done = gathering(FOUR, x)
        for copy in gain_copies:
            copy.wait()
        lax.fori_loop(0, 4 * 32, repack_four, 0)

        def step(s, carry, ready=True):
            cs[s] = c_out[...]
            c_out[...] = forward(s, s, ready)
            return carry

        @pl.when(j == 1)
        def _():
            fwd.wait_recv()
            c_out[...] = c_in[...]
            lax.fori_loop(0, 4, lambda s, carry: step(s, carry, False), 0)
            pl.semaphore_wait(barrier, 1)
            fwd.start()
            lax.fori_loop(0, 40, transpose, 0)

        @pl.when(j > 1)
        def _():
            lax.fori_loop(0, 40, transpose, 0)
            fwd.wait_recv()
            c_out[...] = c_in[...]
            lax.fori_loop(0, 4, step, 0)

            @pl.when(j < 3)
            def _():
                pl.semaphore_wait(barrier, 1)
                fwd.start()

        sends_done()

    ex = [
        remote(acts.at[:, 1 - c], acts_o, ex_s.at[0], ex_r.at[0], core_partner),
        remote(cs, cs_o, ex_s.at[1], ex_r.at[1], core_partner),
    ]

    @pl.when(j < 3)
    def _():
        ex[0].start()
        ex[1].start()

    def ex_dpre(s):
        return remote(dpre.at[s, 1 - c], dpre_o.at[s], ex_s.at[2 + s], ex_r.at[2 + s], core_partner)

    def ex_grad(s):
        return remote(gs.at[s], gs_o.at[s], ex_s.at[6 + s], ex_r.at[6 + s], core_partner)

    def backward(i, s):
        grad = gs[i]
        e = jnp.dot(grad, wt[s], preferred_element_type=F32) * dn[i]
        hat = xh[i]
        dp = (e - hat * jnp.mean(e * hat, axis=1, keepdims=True)).astype(BF)
        dpre[i, 0] = dp[:, :HALF]
        dpre[i, 1] = dp[:, HALF:]
        return (grad.astype(F32) + jnp.dot(dp, w[s], preferred_element_type=F32)).astype(BF)

    rows = pl.ds(pl.multiple_of(x * T, T), T)
    sg_copies = [
        remote(x_back.at[lax.rem(x + i, 4)], sg_ref.at[0, rows], sg_s.at[i - 1], sg_r.at[i - 1], beside[i - 1])
        for i in (1, 2, 3)
    ]

    @pl.when(j == 0)
    def _():
        def step(m, carry):
            down(m).wait_recv()
            grad = backward(m, 0)
            x_back[m] = grad

            @pl.when(x > 0)
            def _():
                down(m).start()

            ex_grad(m).start()
            ex_dpre(m).start()
            sg_ref[0, pl.ds(pl.multiple_of(m * T, T), T), :] = grad
            return carry

        lax.fori_loop(0, 4, step, 0)

    @pl.when(j > 0)
    def _():
        @pl.when(j == 3)
        def _():
            g_out[...] = cot_ref[rows, :]

        @pl.when(j < 3)
        def _():
            bwd.wait_recv()
            g_out[...] = g_in[...]

        def step(i, carry):
            s = 3 - i
            gs[s] = g_out[...]
            grad = backward(s, s)
            g_out[...] = grad

            @pl.when((i == 3) & (j == 1))
            def _():
                bwd_last.start()

            @pl.when((i == 3) & (j > 1))
            def _():
                bwd.start()

            x_back[s] = grad
            ex_grad(s).start()
            ex_dpre(s).start()
            return carry

        lax.fori_loop(0, 4, step, 0)

        sg_ref[0, rows, :] = x_back[x]
        for copy in sg_copies:
            copy.start()

    @pl.when(j == 3)
    def _():
        ex[0].start()
        ex[1].start()

    ex[0].wait_recv()
    ex[1].wait_recv()

    def left_of(i, at):
        return [dpre[i, c, :, at], dpre_o[i, :, at], acts[i, c, :, at], acts_o[i, :, at]]

    def right_of(i):
        return [cs[i], cs_o[i], gs[i], gs_o[i]]

    def outer(left, right):
        left, right = jnp.concatenate(left, axis=0), jnp.concatenate(right, axis=0)
        return lax.dot_general(left, right, (((0,), (0,)), ((), ())), preferred_element_type=F32).astype(BF)

    def summing(orders, s):
        steps = len(orders[0][0])

        def own(h, p):
            return place(orders[p][h], s, zl, y, 0)

        def reduce(h, p, step):
            n = 1 << step
            return remote(
                g.at[p, pl.ds(other(own(h, p), step), n), STREAMS[h]],
                r.at[p, pl.ds(n - 1, n), STREAMS[h]],
                rs_s.at[step, p, h], rs_r.at[step, p, h], partner[orders[p][h][step]],
            )

        for unit in UNITS:
            reduce(*unit, steps - 1).start()
        for step in range(steps - 1, -1, -1):
            for h, p in UNITS:
                n = 1 << step
                base = held(own(h, p), step)
                reduce(h, p, step).wait_recv()

                def add(start, count, p=p, h=h, n=n, base=base):
                    def one(i, carry):
                        at = start + i
                        g[p, at, STREAMS[h]] = g[p, at, STREAMS[h]] + r[p, n - 1 + at - base, STREAMS[h]]
                        return carry

                    lax.fori_loop(0, count, one, 0, unroll=min(count, 8))

                if step:
                    add(other(own(h, p), step - 1), n // 2)
                    reduce(h, p, step - 1).start()
                    add(held(own(h, p), step - 1), n // 2)
                else:
                    add(base, 1)

        for h, p in UNITS:
            total = g[p, own(h, p), STREAMS[h]].astype(F32)
            wg_ref[0, STREAMS[h], p * LANES:(p + 1) * LANES] = total * (1.0 / math.sqrt(8192))
        for unit in UNITS:
            for step in range(steps):
                reduce(*unit, step).wait_send()

    @pl.when(j == 0)
    def _():
        right = []
        for m in range(4):
            ex_grad(m).wait_recv()
            ex_dpre(m).wait_recv()
            right += right_of(m)
        for zh in range(2):
            at = slice(zh * 640, zh * 640 + 640)
            grad = outer([v for m in range(4) for v in left_of(m, at)], right)
            for t in range(8):
                for h, p in UNITS:
                    rows = STREAMS[h]
                    to = place(ONE[p][h], x, 2 * zh + t // 4, t % 4, 0)
                    g[p, to, rows] = grad[t * ROWS + rows.start:t * ROWS + rows.stop, p * LANES:(p + 1) * LANES]
        summing(ONE, x)

    @pl.when(j > 0)
    def _():
        def section(i, carry):
            s = 3 - i
            ex_grad(s).wait_recv()
            ex_dpre(s).wait_recv()
            for zh in range(2):
                grad = outer(left_of(s, slice(zh * 640, zh * 640 + 640)), right_of(s))
                for t in range(8):
                    for p in range(PLANS):
                        to = place(FOUR[p][0], s, 2 * zh + t // 4, t % 4, 0)
                        g[p, to] = grad[t * ROWS:(t + 1) * ROWS, p * LANES:(p + 1) * LANES]
            return carry

        lax.fori_loop(0, 4, section, 0)
        summing(FOUR, x)
        for copy in sg_copies:
            copy.wait()

    ex[0].wait_send()
    ex[1].wait_send()

    def sent(s, carry):
        ex_grad(s).wait_send()
        ex_dpre(s).wait_send()
        return carry

    lax.fori_loop(0, 4, sent, 0)

    @pl.when(j < 3)
    def _():
        fwd.wait_send()

    @pl.when(j > 0)
    def _():
        bwd.wait_send()

    @pl.when(j == 0)
    def _():
        def sent(m, carry):
            @pl.when(x < 3)
            def _():
                up(m).wait_send()

            @pl.when((x == 3) & (m < 3))
            def _():
                relay(m).wait_send()

            @pl.when(x > 0)
            def _():
                down(m).wait_send()

            return carry

        lax.fori_loop(0, 4, sent, 0)


def shards(boundary_in, weights, gains, cotangent):
    vmem = pl.BlockSpec(memory_space=pltpu.VMEM)
    dma = pltpu.SemaphoreType.DMA
    return pl.pallas_call(
        kernel,
        out_shape=(
            jax.ShapeDtypeStruct((1, ROWS, C), F32),
            jax.ShapeDtypeStruct((1, 4 * T, C), BF),
        ),
        in_specs=[vmem] * 4,
        out_specs=(vmem, vmem),
        scratch_shapes=[
            pltpu.VMEM((PLANS, BLOCKS, ROWS, LANES), BF),
            pltpu.VMEM((PLANS, BLOCKS // 2 - 1, ROWS, LANES), BF),
            pltpu.VMEM((4, H, C), BF),
            pltpu.VMEM((4, C, H), BF),
            pltpu.VMEM((4, 1, H), F32),
            pltpu.VMEM((4, T, H), F32),
            pltpu.VMEM((4, T, H), F32),
            pltpu.VMEM((4, 2, T, HALF), BF),
            pltpu.VMEM((4, T, HALF), BF),
            pltpu.VMEM((4, 2, T, HALF), BF),
            pltpu.VMEM((4, T, HALF), BF),
            pltpu.VMEM((4, T, C), BF),
            pltpu.VMEM((4, T, C), BF),
            pltpu.VMEM((4, T, C), BF),
            pltpu.VMEM((4, T, C), BF),
            pltpu.VMEM((T, C), BF),
            pltpu.VMEM((T, C), BF),
            pltpu.VMEM((T, C), BF),
            pltpu.VMEM((T, C), BF),
            pltpu.VMEM((4, T, C), BF),
            pltpu.VMEM((4, T, C), BF),
            dma((6, PLANS, 2)),
            dma((6, PLANS, 2)),
            dma((2, PLANS, 2)),
            dma((2, PLANS, 2)),
            dma((6, PLANS, 2)),
            dma((6, PLANS, 2)),
            dma((3,)),
            dma((3,)),
            dma((2,)),
            dma((2,)),
            dma((3,)),
            dma((3,)),
            dma((10,)),
            dma((10,)),
            dma((4,)),
            dma((4,)),
            dma((4,)),
            dma((4,)),
            dma((3,)),
            dma((1,)),
        ],
        compiler_params=pltpu.CompilerParams(
            collective_id=0, has_side_effects=True, vmem_limit_bytes=60 << 20
        ),
    )(boundary_in, weights, gains, cotangent)


def solution(mesh):
    return jax.shard_map(
        shards,
        mesh=mesh,
        in_specs=(P("dp", None), P("section", "dp", None), P("section", None), P("dp", None)),
        out_specs=(P("section", "dp", None), P("section", "dp", None)),
        check_vma=False,
    )
```

time: 199 us -> 185 us (0.930); the launches traced: 196 us -> 185 us
  Pallas kernels: 193 us -> 182 us
    pallas_call x1, Pallas kernels: 193 us -> 182 us  [shards(): pl.pallas_call(kernel, out_shape=(jax.ShapeDtypeStruct((1, ROWS, C), F32)...]
where the time goes in v3:
time: 185 us
  Pallas kernels  182 us (98%)
  local copies, waits for them, and re-layouts  2.4 us (1%)
    pallas_call x1, Pallas kernels, shards(): pl.pallas_call(kernel, out_shape=(jax.ShapeDtypeStruct((1, ROWS, C), F32)...  182 us

profile of v3, /device:TPU:1, one launch (start us, length us, event | category | flops | bytes accessed | tf_op | source)
XLA Modules:
  0.0 185.2 jit_solution(1130019282330369518)
XLA Ops:
  0.6 182.1 %shard_map.59 = (f32[1,80,640]{2,1,0:T(8,128)}, bf16[1,256,640]{2,1,0:T(8,128)(2,1)}) custom-call(bf16[256,640]{1,0:T(8,128)(2,1)} %b_ref.1, bf16[1,80,640]{2,1,0:T(8,128)(2,1)} %w_ref.1, f32[1,2560]{1,0:T(1,128)} %gain_ref.1, bf16[256,640]{1,0:T(8,128)(2,1)} %cot_ref.1), custom_call_target="tpu_custom_call" | custom-call | tf_op jit(solution)/shard_map/pallas_call | solution.py:527
  182.8 0.0 copy-start
  182.8 1.7 copy.8
  184.5 0.0 copy-done
  184.5 0.7 copy.9
Async XLA Ops:
  182.8 1.7 copy-start

commit v4 on v3

--- a/solution.py
+++ b/solution.py
@@ -15,6 +15,7 @@
 BLOCKS = 128
 HALF = H // 2
 STREAMS = (slice(0, 48), slice(48, 80))
+COLS = (slice(0, 256), slice(256, C))
 UNITS = [(h, p) for h in range(2) for p in range(PLANS)]
 
 _FOUR, _ONE = ["xu", "yu", "za", "xv", "yv"], ["yu", "za", "yv"]
@@ -38,8 +39,8 @@
 
 def kernel(b_ref, w_ref, gain_ref, cot_ref, wg_ref, sg_ref,
            g, r, w, wt, gains, xh, dn, acts, acts_o, dpre, dpre_o, cs, cs_o, gs, gs_o,
-           c_in, c_out, g_in, g_out, x_send, x_back,
-           ag_s, ag_r, co_s, co_r, rs_s, rs_r, gn_s, gn_r, hop_s, hop_r, sg_s, sg_r, ex_s, ex_r,
+           c_in, c_out, g_out, x_send, x_back,
+           ag_s, ag_r, co_s, co_r, rs_s, rs_r, gn_s, gn_r, hop_s, sg_s, sg_r, ex_s, ex_r,
            up_s, up_r, down_s, down_r, relay_s, relay_r):
     sec, dp = lax.axis_index("section"), lax.axis_index("dp")
     j, x = lax.div(sec, 4), lax.rem(sec, 4)
@@ -129,9 +130,18 @@
         def own(h, p):
             return place(orders[p][h], s, zl, y, c)
 
-        def gather(h, p, step):
-            part = g.at[p, pl.ds(held(own(h, p), step), 1 << step), STREAMS[h]]
-            return remote(part, part, ag_s.at[step, p, h], ag_r.at[step, p, h], partner[orders[p][h][step]])
+        def gather(h, p, step, late):
+            if step:
+                first, n = (other if late else held)(own(h, p), step - 1), 1 << (step - 1)
+            else:
+                first, n = own(h, p), 1
+            part = g.at[p, pl.ds(first, n), STREAMS[h]]
+            return remote(part, part, ag_s.at[step, late, p, h], ag_r.at[step, late, p, h], partner[orders[p][h][step]])
+
+        def arrive(h, p, step):
+            if step:
+                gather(h, p, step, 0).wait_recv()
+            gather(h, p, step, 1).wait_recv()
 
         def across(h, p, late):
             first = (other if late else held)(own(h, p), steps - 1)
@@ -139,15 +149,19 @@
             return remote(part, part, co_s.at[late, p, h], co_r.at[late, p, h], core_partner)
 
         for unit in UNITS:
-            gather(*unit, 0).start()
+            gather(*unit, 0, 1).start()
+        for unit in UNITS:
+            gather(*unit, 1, 0).start()
         for step in range(1, steps):
             for unit in UNITS:
-                gather(*unit, step - 1).wait_recv()
-                gather(*unit, step).start()
+                arrive(*unit, step - 1)
+                gather(*unit, step, 1).start()
+                if step + 1 < steps:
+                    gather(*unit, step + 1, 0).start()
         for unit in UNITS:
             across(*unit, 0).start()
         for unit in UNITS:
-            gather(*unit, steps - 1).wait_recv()
+            arrive(*unit, steps - 1)
             across(*unit, 1).start()
         for unit in UNITS:
             across(*unit, 0).wait_recv()
@@ -156,7 +170,9 @@
         def sends_done():
             for unit in UNITS:
                 for step in range(steps):
-                    gather(*unit, step).wait_send()
+                    if step:
+                        gather(*unit, step, 0).wait_send()
+                    gather(*unit, step, 1).wait_send()
                 across(*unit, 0).wait_send()
                 across(*unit, 1).wait_send()
 
@@ -189,36 +205,64 @@
         wt[s, :, at] = w[s, at, :].T
         return carry
 
-    fwd = remote(c_out, c_in, hop_s.at[0], hop_r.at[0], ahead)
-    bwd = remote(g_out, g_in, hop_s.at[1], hop_r.at[1], behind)
-    bwd_last = remote(g_out, gs.at[x], hop_s.at[1], down_r.at[x], last)
-
-    def up(m):
-        return remote(x_send.at[m], cs.at[m], up_s.at[m], up_r.at[m], device(j, lax.rem(x + 1, 4), zl, y, c))
-
-    def down(m):
-        return remote(x_back.at[m], gs.at[m], down_s.at[m], down_r.at[m], device(j, lax.rem(x + 3, 4), zl, y, c))
-
-    def relay(m):
-        return remote(x_send.at[m], c_in, relay_s.at[m], relay_r.at[0], device(j, m, zl, y, c))
-
-    def forward(i, s, ready=True):
-        block = cs[i]
+    def hop(src, dst, sems, i, part, to):
+        cols = COLS[part]
+        return remote(src.at[:, cols], dst.at[:, cols], sems[0].at[i, part], sems[1].at[i, part], to)
+
+    UP, DOWN = (up_s, up_r), (down_s, down_r)
+
+    def fwd(part, src):
+        return hop(src, cs.at[0], (hop_s, up_r), 0, part, ahead)
+
+    def bwd(part):
+        return hop(g_out, gs.at[3], (hop_s, down_r), 1, part, behind)
+
+    def bwd_last(part):
+        cols = COLS[part]
+        return remote(g_out.at[:, cols], gs.at[x, :, cols], hop_s.at[1, part], down_r.at[x, part], last)
+
+    def up(m, part):
+        return hop(x_send.at[m], cs.at[m], UP, m, part, device(j, lax.rem(x + 1, 4), zl, y, c))
+
+    def down(m, part):
+        return hop(x_back.at[m], gs.at[m], DOWN, m, part, device(j, lax.rem(x + 3, 4), zl, y, c))
+
+    def relay(m, part):
+        cols = COLS[part]
+        return remote(x_send.at[m, :, cols], c_in.at[:, cols], relay_s.at[m, part], relay_r.at[0, part], device(j, m, zl, y, c))
+
+    def by_parts(value, weight, arrived):
+        if arrived is None:
+            return jnp.dot(value[...], weight[...], preferred_element_type=F32)
+        arrived(0)
+        total = jnp.dot(value[:, COLS[0]], weight[COLS[0], :], preferred_element_type=F32)
+        arrived(1)
+        return total + jnp.dot(value[:, COLS[1]], weight[COLS[1], :], preferred_element_type=F32)
+
+    def leave(block, change, s, send):
+        for part, cols in enumerate(COLS):
+            out = block[:, cols].astype(F32) + jnp.dot(change, w[s, :, cols], preferred_element_type=F32)
+            send(part, out.astype(BF))
+
+    def forward(i, s, send, arrived=None, ready=True):
         if ready:
-            pre = jnp.dot(block, wt[s], preferred_element_type=F32)
+            pre = by_parts(cs.at[i], wt.at[s], arrived)
         else:
-            pre = lax.dot_general(block, w[s], (((1,), (1,)), ((), ())), preferred_element_type=F32)
+            if arrived is not None:
+                arrived(0)
+                arrived(1)
+            pre = lax.dot_general(cs[i], w[s], (((1,), (1,)), ((), ())), preferred_element_type=F32)
         inv = lax.rsqrt(jnp.mean(pre * pre, axis=1, keepdims=True) + 1e-05)
         hat = pre * inv
         gain = gains[s]
         normed = hat * gain
         sig = 1.0 / (1.0 + jnp.exp(-normed))
         act = (normed * sig).astype(BF)
+        leave(cs.at[i], act, s, send)
         xh[i] = hat
         dn[i] = sig * (1.0 + normed * (1.0 - sig)) * gain * inv
         acts[i, 0] = act[:, :HALF]
         acts[i, 1] = act[:, HALF:]
-        return (block.astype(F32) + jnp.dot(act, w[s], preferred_element_type=F32)).astype(BF)
 
     @pl.when(j == 0)
     def _():
@@ -232,35 +276,37 @@
                 cs[m] = b_ref[m * T:(m + 1) * T, :]
 
         def step(m, carry):
-            @pl.when(x > 0)
+            def arrived(part):
+                @pl.when(x > 0)
+                def _():
+                    up(m, part).wait_recv()
+
+            def send(part, value):
+                x_send[m, :, COLS[part]] = value
+
+                @pl.when(x < 3)
+                def _():
+                    up(m, part).start()
+
+                @pl.when((x == 3) & (m < 3))
+                def _():
+                    relay(m, part).start()
+
+            forward(m, 0, send, arrived)
+            return carry
+
+        lax.fori_loop(0, 4, step, 0)
+        pl.semaphore_wait(barrier, 1)
+        for part in range(2):
+            @pl.when(x == 3)
             def _():
-                up(m).wait_recv()
-
-            x_send[m] = forward(m, 0)
+                fwd(part, x_send.at[3]).start()
 
             @pl.when(x < 3)
             def _():
-                up(m).start()
-
-            @pl.when((x == 3) & (m < 3))
-            def _():
-                relay(m).start()
-
-            return carry
-
-        lax.fori_loop(0, 4, step, 0)
-
-        @pl.when(x == 3)
-        def _():
-            c_out[...] = x_send[3]
-
-        @pl.when(x < 3)
-        def _():
-            relay(0).wait_recv()
-            c_out[...] = c_in[...]
-
-        pl.semaphore_wait(barrier, 1)
-        fwd.start()
+                relay(0, part).wait_recv()
+                fwd(part, c_in).start()
+
         sends_done()
 
     @pl.when(j > 0)
@@ -272,31 +318,49 @@
             copy.wait()
         lax.fori_loop(0, 4 * 32, repack_four, 0)
 
-        def step(s, carry, ready=True):
-            cs[s] = c_out[...]
-            c_out[...] = forward(s, s, ready)
-            return carry
-
-        @pl.when(j == 1)
-        def _():
-            fwd.wait_recv()
-            c_out[...] = c_in[...]
-            lax.fori_loop(0, 4, lambda s, carry: step(s, carry, False), 0)
-            pl.semaphore_wait(barrier, 1)
-            fwd.start()
-            lax.fori_loop(0, 40, transpose, 0)
-
-        @pl.when(j > 1)
-        def _():
-            lax.fori_loop(0, 40, transpose, 0)
-            fwd.wait_recv()
-            c_out[...] = c_in[...]
-            lax.fori_loop(0, 4, step, 0)
+        def arrived(part):
+            fwd(part, c_out).wait_recv()
+
+        def stage(ready):
+            def within(s, carry):
+                def send(part, value):
+                    cs[s + 1, :, COLS[part]] = value
+
+                forward(s, s, send, ready=ready)
+                return carry
+
+            def send(part, value):
+                c_out[:, COLS[part]] = value
+                fwd(part, c_out).start()
+
+            def end(part, value):
+                pass
+
+            def first(part, value):
+                cs[1, :, COLS[part]] = value
+
+            forward(0, 0, first, arrived, ready)
+            lax.fori_loop(1, 3, within, 0)
 
             @pl.when(j < 3)
             def _():
                 pl.semaphore_wait(barrier, 1)
-                fwd.start()
+                forward(3, 3, send, ready=ready)
+
+            if ready:
+                @pl.when(j == 3)
+                def _():
+                    forward(3, 3, end)
+
+        @pl.when(j == 1)
+        def _():
+            stage(False)
+            lax.fori_loop(0, 40, transpose, 0)
+
+        @pl.when(j > 1)
+        def _():
+            lax.fori_loop(0, 40, transpose, 0)
+            stage(True)
 
         sends_done()
 
@@ -316,14 +380,15 @@
     def ex_grad(s):
         return remote(gs.at[s], gs_o.at[s], ex_s.at[6 + s], ex_r.at[6 + s], core_partner)
 
-    def backward(i, s):
-        grad = gs[i]
-        e = jnp.dot(grad, wt[s], preferred_element_type=F32) * dn[i]
+    def backward(i, s, send, arrived=None):
+        e = by_parts(gs.at[i], wt.at[s], arrived) * dn[i]
         hat = xh[i]
         dp = (e - hat * jnp.mean(e * hat, axis=1, keepdims=True)).astype(BF)
+        leave(gs.at[i], dp, s, send)
         dpre[i, 0] = dp[:, :HALF]
         dpre[i, 1] = dp[:, HALF:]
-        return (grad.astype(F32) + jnp.dot(dp, w[s], preferred_element_type=F32)).astype(BF)
+        ex_grad(i).start()
+        ex_dpre(i).start()
 
     rows = pl.ds(pl.multiple_of(x * T, T), T)
     sg_copies = [
@@ -334,53 +399,63 @@
     @pl.when(j == 0)
     def _():
         def step(m, carry):
-            down(m).wait_recv()
-            grad = backward(m, 0)
-            x_back[m] = grad
-
-            @pl.when(x > 0)
+            def arrived(part):
+                down(m, part).wait_recv()
+
+            def send(part, value):
+                x_back[m, :, COLS[part]] = value
+
+                @pl.when(x > 0)
+                def _():
+                    down(m, part).start()
+
+            backward(m, 0, send, arrived)
+            sg_ref[0, pl.ds(pl.multiple_of(m * T, T), T), :] = x_back[m]
+            return carry
+
+        lax.fori_loop(0, 4, step, 0)
+
+    @pl.when(j > 0)
+    def _():
+        @pl.when(j == 3)
+        def _():
+            gs[3] = cot_ref[rows, :]
+
+        def arrived(part):
+            @pl.when(j < 3)
             def _():
-                down(m).start()
-
-            ex_grad(m).start()
-            ex_dpre(m).start()
-            sg_ref[0, pl.ds(pl.multiple_of(m * T, T), T), :] = grad
-            return carry
-
-        lax.fori_loop(0, 4, step, 0)
-
-    @pl.when(j > 0)
-    def _():
-        @pl.when(j == 3)
-        def _():
-            g_out[...] = cot_ref[rows, :]
-
-        @pl.when(j < 3)
-        def _():
-            bwd.wait_recv()
-            g_out[...] = g_in[...]
+                bwd(part).wait_recv()
+
+        def first(part, value):
+            gs[2, :, COLS[part]] = value
+            x_back[3, :, COLS[part]] = value
 
         def step(i, carry):
             s = 3 - i
-            gs[s] = g_out[...]
-            grad = backward(s, s)
-            g_out[...] = grad
-
-            @pl.when((i == 3) & (j == 1))
+
+            def send(part, value):
+                gs[s - 1, :, COLS[part]] = value
+                x_back[s, :, COLS[part]] = value
+
+            backward(s, s, send)
+            return carry
+
+        def out(part, value):
+            g_out[:, COLS[part]] = value
+
+            @pl.when(j == 1)
             def _():
-                bwd_last.start()
-
-            @pl.when((i == 3) & (j > 1))
+                bwd_last(part).start()
+
+            @pl.when(j > 1)
             def _():
-                bwd.start()
-
-            x_back[s] = grad
-            ex_grad(s).start()
-            ex_dpre(s).start()
-            return carry
-
-        lax.fori_loop(0, 4, step, 0)
-
+                bwd(part).start()
+
+            x_back[0, :, COLS[part]] = value
+
+        backward(3, 3, first, arrived)
+        lax.fori_loop(1, 3, step, 0)
+        backward(0, 0, out)
         sg_ref[0, rows, :] = x_back[x]
         for copy in sg_copies:
             copy.start()
@@ -493,28 +568,30 @@
 
     lax.fori_loop(0, 4, sent, 0)
 
-    @pl.when(j < 3)
-    def _():
-        fwd.wait_send()
-
-    @pl.when(j > 0)
-    def _():
-        bwd.wait_send()
+    for part in range(2):
+        @pl.when(j < 3)
+        def _():
+            fwd(part, c_out).wait_send()
+
+        @pl.when(j > 0)
+        def _():
+            bwd(part).wait_send()
 
     @pl.when(j == 0)
     def _():
         def sent(m, carry):
-            @pl.when(x < 3)
-            def _():
-                up(m).wait_send()
-
-            @pl.when((x == 3) & (m < 3))
-            def _():
-                relay(m).wait_send()
-
-            @pl.when(x > 0)
-            def _():
-                down(m).wait_send()
+            for part in range(2):
+                @pl.when(x < 3)
+                def _():
+                    up(m, part).wait_send()
+
+                @pl.when((x == 3) & (m < 3))
+                def _():
+                    relay(m, part).wait_send()
+
+                @pl.when(x > 0)
+                def _():
+                    down(m, part).wait_send()
 
             return carry
 
@@ -551,29 +628,27 @@
             pltpu.VMEM((T, C), BF),
             pltpu.VMEM((T, C), BF),
             pltpu.VMEM((T, C), BF),
-            pltpu.VMEM((T, C), BF),
             pltpu.VMEM((4, T, C), BF),
             pltpu.VMEM((4, T, C), BF),
-            dma((6, PLANS, 2)),
-            dma((6, PLANS, 2)),
+            dma((6, 2, PLANS, 2)),
+            dma((6, 2, PLANS, 2)),
             dma((2, PLANS, 2)),
             dma((2, PLANS, 2)),
             dma((6, PLANS, 2)),
             dma((6, PLANS, 2)),
             dma((3,)),
             dma((3,)),
-            dma((2,)),
-            dma((2,)),
+            dma((2, 2)),
             dma((3,)),
             dma((3,)),
             dma((10,)),
             dma((10,)),
-            dma((4,)),
-            dma((4,)),
-            dma((4,)),
-            dma((4,)),
-            dma((3,)),
-            dma((1,)),
+            dma((4, 2)),
+            dma((4, 2)),
+            dma((4, 2)),
+            dma((4, 2)),
+            dma((3, 2)),
+            dma((1, 2)),
         ],
         compiler_params=pltpu.CompilerParams(
             collective_id=0, has_side_effects=True, vmem_limit_bytes=60 << 20

time: 185 us -> 184 us (level)
  Pallas kernels: 182 us -> 180 us
where the time goes in v4:
time: 184 us; the launch traced here: 183 us
  Pallas kernels  180 us (98%)
  local copies, waits for them, and re-layouts  2.4 us (1%)
    pallas_call x1, Pallas kernels, shards(): pl.pallas_call(kernel, out_shape=(jax.ShapeDtypeStruct((1, ROWS, C), F32)...  180 us

profile of v4, /device:TPU:1, one launch (start us, length us, event | category | flops | bytes accessed | tf_op | source)
XLA Modules:
  0.0 183.3 jit_solution(1297254728938417864)
XLA Ops:
  0.6 180.3 %shard_map.59 = (f32[1,80,640]{2,1,0:T(8,128)}, bf16[1,256,640]{2,1,0:T(8,128)(2,1)}) custom-call(bf16[256,640]{1,0:T(8,128)(2,1)} %b_ref.1, bf16[1,80,640]{2,1,0:T(8,128)(2,1)} %w_ref.1, f32[1,2560]{1,0:T(1,128)} %gain_ref.1, bf16[256,640]{1,0:T(8,128)(2,1)} %cot_ref.1), custom_call_target="tpu_custom_call" | custom-call | tf_op jit(solution)/shard_map/pallas_call | solution.py:604
  180.9 0.0 copy-start
  181.0 1.7 copy.8
  182.6 0.0 copy-done
  182.6 0.7 copy.9
Async XLA Ops:
  180.9 1.7 copy-start

commit v5 on v4

--- a/solution.py
+++ b/solution.py
@@ -158,8 +158,8 @@
                 gather(*unit, step, 1).start()
                 if step + 1 < steps:
                     gather(*unit, step + 1, 0).start()
-        for unit in UNITS:
-            across(*unit, 0).start()
+                else:
+                    across(*unit, 0).start()
         for unit in UNITS:
             arrive(*unit, steps - 1)
             across(*unit, 1).start()

time: 184 us -> 185 us (level)
  Pallas kernels: 180 us -> 182 us
where the time goes in v5:
time: 185 us
  Pallas kernels  182 us (98%)
  local copies, waits for them, and re-layouts  2.4 us (1%)
    pallas_call x1, Pallas kernels, shards(): pl.pallas_call(kernel, out_shape=(jax.ShapeDtypeStruct((1, ROWS, C), F32)...  182 us

profile of v5, /device:TPU:1, one launch (start us, length us, event | category | flops | bytes accessed | tf_op | source)
XLA Modules:
  0.0 184.7 jit_solution(15969292695976554381)
XLA Ops:
  0.6 181.6 %shard_map.59 = (f32[1,80,640]{2,1,0:T(8,128)}, bf16[1,256,640]{2,1,0:T(8,128)(2,1)}) custom-call(bf16[256,640]{1,0:T(8,128)(2,1)} %b_ref.1, bf16[1,80,640]{2,1,0:T(8,128)(2,1)} %w_ref.1, f32[1,2560]{1,0:T(1,128)} %gain_ref.1, bf16[256,640]{1,0:T(8,128)(2,1)} %cot_ref.1), custom_call_target="tpu_custom_call" | custom-call | tf_op jit(solution)/shard_map/pallas_call | solution.py:604
  182.3 0.0 copy-start
  182.3 1.7 copy.8
  183.9 0.0 copy-done
  183.9 0.7 copy.9
Async XLA Ops:
  182.3 1.7 copy-start
